TPU v7x, 32 devices: a whole 2x2x4 slice. The times are simulated.
32 devices in a mesh: ctx: 16 (over z, y, x), tp: 2 (over core).
Axes of the slice: x: 2, y: 2, z: 4, core: 2. Of those that a mesh axis runs over, the one named last changes fastest.
Arguments:
- features: bfloat16 [3, 2048, 2048], P(None, 'tp', 'ctx'), may hold values from -6 to 6
- short_taps: float32 [7, 3, 2048], P(None, None, 'tp'), may hold values from -2.5 to 2.5
- long_filter: float32 [2048, 2048], P('tp', 'ctx'), may hold values from -0.125 to 0.125
- skip: float32 [2048], P('tp'), may hold values from 0.25 to 1.5
- norm_gain: float32 [2048], replicated, may hold values from 0.1 to 1.9
- w_qkv: bfloat16 [2048, 3, 2048], P('ctx', None, 'tp'), may hold values from -1 to 1
Outputs:
- mixed: bfloat16 [2048, 2048], P('tp', 'ctx')
- attended: bfloat16 [2048, 2048], P('ctx', 'tp')
All inputs are finite; a program needn't handle non-finite values.
Results may differ from a plain program's by a relative error of at most 0.02.
Values may be sent and summed in bfloat16 or wider, within the bound.
A program may use at most 128 MiB of HBM per device.

v0:
```python
import math

import jax
import jax.numpy as jnp
from jax import lax
from jax.sharding import PartitionSpec as P

DH = 128


HIGHEST = lax.Precision.HIGHEST


def shifted(block, axis, distance):
    devices = range(lax.axis_size(axis))
    route = [(i - distance, i) for i in devices if i - distance in devices]
    return lax.ppermute(block, axis, route)


def angle_table(rows, cols, modulus):
    left = jnp.arange(rows, dtype=jnp.int32)[:, None]
    right = jnp.arange(cols, dtype=jnp.int32)[None, :]
    phase = (left * right % modulus).astype(jnp.float32) * (2.0 * math.pi / modulus)
    return (jnp.cos(phase), jnp.sin(phase))


def contract(form, data, table):
    return jnp.einsum(form, data, table, precision=HIGHEST)


def spectrum(lanes, tok):
    width = lanes.shape[0]
    length = lanes.shape[1]
    outer = 2 * tok
    inner = 2 * length // outer
    data = lanes.reshape(width, tok, inner)
    cos_a, sin_a = angle_table(tok, outer, outer)
    first_re = contract("kaq,ab->kbq", data, cos_a)
    first_im = -contract("kaq,ab->kbq", data, sin_a)
    cos_t, sin_t = angle_table(outer, inner, 2 * length)
    turned_re = first_re * cos_t + first_im * sin_t
    turned_im = first_im * cos_t - first_re * sin_t
    cos_b, sin_b = angle_table(inner, inner, inner)
    out_re = contract("kbq,qr->kbr", turned_re, cos_b) + contract("kbq,qr->kbr", turned_im, sin_b)
    out_im = contract("kbq,qr->kbr", turned_im, cos_b) - contract("kbq,qr->kbr", turned_re, sin_b)
    return (out_re, out_im)


def inverse_real(spec_re, spec_im, tok, length):
    width = spec_re.shape[0]
    outer = 2 * tok
    inner = spec_re.shape[2]
    cos_b, sin_b = angle_table(inner, inner, inner)
    back_re = contract("kbr,rq->kbq", spec_re, cos_b) - contract("kbr,rq->kbq", spec_im, sin_b)
    back_im = contract("kbr,rq->kbq", spec_im, cos_b) + contract("kbr,rq->kbq", spec_re, sin_b)
    cos_t, sin_t = angle_table(outer, inner, 2 * length)
    turned_re = back_re * cos_t - back_im * sin_t
    turned_im = back_im * cos_t + back_re * sin_t
    cos_a, sin_a = angle_table(outer, tok, outer)
    real = contract("kbq,ba->kaq", turned_re, cos_a) - contract("kbq,ba->kaq", turned_im, sin_a)
    return (real / (2 * length)).reshape(width, length)


def attend_rows(query_rows, query_pos, keyvals, count, block):
    rows = query_rows.shape[0]
    scale = DH ** (-0.5)
    start_state = (
        jnp.full((rows,), -1e30, jnp.float32),
        jnp.zeros((rows,), jnp.float32),
        jnp.zeros((rows, DH), jnp.float32),
    )

    def step(index, state):
        running, total, accum = state
        part = lax.dynamic_slice_in_dim(keyvals, index * block, block, 0)
        keys = part[:, :DH]
        vals = part[:, DH:]
        scores = (
            lax.dot_general(
                query_rows, keys, (((1,), (1,)), ((), ())), preferred_element_type=jnp.float32
            )
            * scale
        )
        key_pos = index * block + jnp.arange(block, dtype=jnp.int32)
        allowed = key_pos[None, :] <= query_pos[:, None]
        scores = jnp.where(allowed, scores, -1e30)
        new_top = jnp.maximum(running, jnp.max(scores, axis=1))
        factor = jnp.exp(running - new_top)
        expo = jnp.where(allowed, jnp.exp(scores - new_top[:, None]), 0.0)
        total = total * factor + jnp.sum(expo, axis=1)
        accum = accum * factor[:, None] + jnp.dot(
            expo.astype(jnp.bfloat16), vals, preferred_element_type=jnp.float32
        )
        return (new_top, total, accum)

    running, total, accum = lax.fori_loop(0, count, step, start_state)
    return accum / total[:, None]


def local(features, short_taps, long_filter, skip, norm_gain, w_qkv):
    taps = short_taps.shape[0]
    tok = features.shape[2]
    rim = shifted(features[:, :, tok - (taps - 1) :], "ctx", 1)
    extended = jnp.concatenate([rim, features], axis=2).astype(jnp.float32)
    short = short_taps[0][:, :, None] * extended[:, :, taps - 1 : taps - 1 + tok]
    for lag in range(1, taps):
        short = (
            short
            + short_taps[lag][:, :, None] * extended[:, :, taps - 1 - lag : taps - 1 - lag + tok]
        )
    carried = (short[1] * short[2]).astype(jnp.bfloat16)
    lanes = lax.all_to_all(carried, "ctx", split_axis=0, concat_axis=1, tiled=True).astype(
        jnp.float32
    )
    filt = lax.all_to_all(long_filter, "ctx", split_axis=0, concat_axis=1, tiled=True)
    length = lanes.shape[1]
    data_re, data_im = spectrum(lanes, tok)
    filt_re, filt_im = spectrum(filt, tok)
    conv = inverse_real(
        data_re * filt_re - data_im * filt_im, data_re * filt_im + data_im * filt_re, tok, length
    )
    long_back = lax.all_to_all(
        conv.astype(jnp.bfloat16), "ctx", split_axis=1, concat_axis=0, tiled=True
    )
    mixed = (
        short[0] * (long_back.astype(jnp.float32) + skip[:, None] * carried.astype(jnp.float32))
    ).astype(jnp.bfloat16)
    whole = lax.all_gather(mixed, "tp", axis=0, tiled=True)
    whole_f = whole.astype(jnp.float32)
    inverse = lax.rsqrt(jnp.mean(whole_f * whole_f, axis=0, keepdims=True) + 1e-06)
    normed = (whole_f * inverse * norm_gain[:, None]).astype(jnp.bfloat16)
    columns = w_qkv.shape[1] * w_qkv.shape[2]
    piece = lax.all_gather(w_qkv, "ctx", axis=0, tiled=True)
    count = piece.shape[0]
    projected = lax.dot_general(
        normed,
        piece.reshape(count, columns),
        (((0,), (0,)), ((), ())),
        preferred_element_type=jnp.float32,
    )
    heads = w_qkv.shape[2] // DH
    projected = projected.astype(jnp.bfloat16).reshape(tok, 3, heads, DH)
    ranks = lax.axis_size("ctx")
    subs = ranks // heads
    sub = tok // subs
    key_pairs = jnp.concatenate([projected[:, 1], projected[:, 2]], axis=-1)
    slot = lax.axis_index("ctx") % subs
    queries = jnp.transpose(projected[:, 0].reshape(subs, sub, heads, DH), (2, 0, 1, 3)).reshape(
        ranks, sub, DH
    )
    pairs = jnp.transpose(key_pairs, (1, 0, 2))
    pairs = jnp.broadcast_to(pairs[:, None], (heads, subs, tok, 2 * DH)).reshape(ranks, tok, 2 * DH)
    got_queries = lax.all_to_all(queries, "ctx", split_axis=0, concat_axis=0, tiled=True).reshape(
        ranks * sub, DH
    )
    got_pairs = lax.all_to_all(pairs, "ctx", split_axis=0, concat_axis=0, tiled=True).reshape(
        ranks * tok, 2 * DH
    )
    source = jnp.arange(ranks * sub, dtype=jnp.int32)
    query_pos = source // sub * tok + slot * sub + source % sub
    total_keys = ranks * tok
    block = min(2048, total_keys)
    result = attend_rows(got_queries, query_pos, got_pairs, total_keys // block, block)
    result = result.astype(jnp.bfloat16).reshape(ranks, sub, DH)
    back = lax.all_to_all(result, "ctx", split_axis=0, concat_axis=0, tiled=True)
    attended = jnp.transpose(back.reshape(heads, subs, sub, DH), (1, 2, 0, 3)).reshape(
        tok, heads * DH
    )
    return (mixed, attended)


def solution(mesh):
    in_specs = (
        P(None, "tp", "ctx"),
        P(None, None, "tp"),
        P("tp", "ctx"),
        P("tp"),
        P(),
        P("ctx", None, "tp"),
    )
    out_specs = (P("tp", "ctx"), P("ctx", "tp"))
    return jax.shard_map(local, mesh=mesh, in_specs=in_specs, out_specs=out_specs, check_vma=False)
```

profile of v0, /device:TPU:0, one launch (start us, length us, event | category | flops | bytes accessed | tf_op | source)
XLA Modules:
  0.0 309.8 jit_solution(6990598623668523524)
XLA Ops:
  7.2 2.4 copy.86
  11.4 4.8 %collective-permute-start = (bf16[3,1024,6]{1,2,0:T(8,128)(2,1)S(1)}, bf16[3,1024,6]{1,2,0:T(8,128)(2,1)S(1)}, u32[]{:S(2)}, u32[]{:S(2)}) collective-permute-start(bf16[3,1024,6]{1,2,0:T(8,128)(2,1)S(1)} %copy.98), channel_id=1, source_target_pairs={{0,2},{2,4},{4,6},{6,8},{8,10},{10,12},{12,14},{14,16},{16,18},{18... | collective-permute-start | bytes 110600 | tf_op jit(solution)/shard_map/ppermute | solution.py:17
  19.0 5.9 %fusion.5 = f32[3,1024,128]{2,1,0:T(8,128)S(1)} fusion(f32[3,1024,134]{2,1,0:T(8,128)S(1)} %maximum_convert_fusion, f32[3,1024]{1,0:T(4,128)S(1)} %get-tuple-element.50, f32[3,1024]{1,0:T(4,128)S(1)} %get-tuple-element.51, f32[3,1024]{1,0:T(4,128)S(1)} %get-tuple-element.52, f32[3,1024]{1,0:T(4,128)S(1)} %get-tuple-element.53, ...), kind=kLoop, calls=%fused_computation.9 | loop fusion | flops 5111808 | bytes 12668928 | tf_op jit(solution)/shard_map/add | solution.py:108
  24.9 16.0 %all_to_all.54 = bf16[16,64,128]{2,1,0:T(8,128)(2,1)S(1)} all-to-all(bf16[16,64,128]{2,1,0:T(8,128)(2,1)S(1)} %bitcast.139), channel_id=1, replica_groups=mesh['ctx'=16,'tp'=2] {'ctx'}, dimensions={0} | all-to-all | bytes 524288 | tf_op jit(solution)/shard_map/all_to_all | solution.py:112
  40.9 4.0 %all-to-all-start.1 = ((f32[16,64,128]{2,1,0:T(8,128)}), f32[16,64,128]{2,1,0:T(8,128)S(1)}, u32[]{:S(2)}, u32[]{:S(2)}) async-start(f32[16,64,128]{2,1,0:T(8,128)} %bitcast.11), calls=%async_computation.1 | async-start | bytes 1048576 | tf_op jit(solution)/shard_map/all_to_all | solution.py:115
  46.8 2.1 fusion.63
  49.0 21.0 %all-to-all-done.1 = f32[16,64,128]{2,1,0:T(8,128)S(1)} async-done(((f32[16,64,128]{2,1,0:T(8,128)}), f32[16,64,128]{2,1,0:T(8,128)S(1)}, u32[]{:S(2)}, u32[]{:S(2)}) %all-to-all-start.1) | async-done | bytes 524320 | tf_op jit(solution)/shard_map/all_to_all | solution.py:115
  74.4 3.0 subtract_bitcast_fusion
  82.3 1.8 fusion.36
  89.0 2.0 multiply_subtract_fusion.1
  94.2 1.7 multiply_add_fusion
  95.9 1.9 fusion.22
  97.8 1.9 fusion.17
  100.4 23.8 %all_to_all.55 = bf16[64,16,128]{2,0,1:T(8,128)(2,1)S(1)} all-to-all(bf16[64,16,128]{2,0,1:T(8,128)(2,1)S(1)} %copy.85), channel_id=1, replica_groups=mesh['ctx'=16,'tp'=2] {'ctx'}, dimensions={1} | all-to-all | bytes 524288 | tf_op jit(solution)/shard_map/all_to_all | solution.py:122
  124.5 2.2 all_gather.6
  126.9 100.5 %all-gather.2.cloned.1.call-done = bf16[2048,3,1024]{0,2,1:T(8,128)(2,1)} async-done(((bf16[128,3,1024]{0,2,1:T(8,128)(2,1)}), bf16[2048,3,1024]{0,2,1:T(8,128)(2,1)}) %all-gather.2.cloned.1.call-update) | async-done | bytes 12582928 | tf_op jit(solution)/shard_map/all_gather | solution.py:133
  227.5 9.3 %fusion.11 = bf16[16,8,24,128]{3,1,2,0:T(8,128)(2,1)S(1)} fusion(bf16[2048,3072]{0,1:T(8,128)(2,1)} %bitcast.132, bf16[2048,128]{1,0:T(8,128)(2,1)S(1)} %all_gather.6, f32[2048]{0:T(1024)S(1)} %copy-done.3, f32[128]{0:T(128)S(1)} %add_rsqrt_fusion), kind=kOutput, calls=%fused_computation.32 | convolution fusion | flops 1612054528 | bytes 13902336 | tf_op jit(solution)/shard_map/dot_general | solution.py:135
  237.8 3.5 %all-to-all-start.3 = ((bf16[16,64,128]{2,1,0:T(8,128)(2,1)}), bf16[16,64,128]{2,1,0:T(8,128)(2,1)S(1)}, u32[]{:S(2)}, u32[]{:S(2)}) async-start(bf16[16,64,128]{2,1,0:T(8,128)(2,1)} %bitcast.25), calls=%async_computation.3 | async-start | bytes 524288 | tf_op jit(solution)/shard_map/all_to_all | solution.py:153
  241.6 10.1 %all-to-all-done.3 = bf16[16,64,128]{2,1,0:T(8,128)(2,1)S(1)} async-done(((bf16[16,64,128]{2,1,0:T(8,128)(2,1)}), bf16[16,64,128]{2,1,0:T(8,128)(2,1)S(1)}, u32[]{:S(2)}, u32[]{:S(2)}) %all-to-all-start.3) | async-done | bytes 262176 | tf_op jit(solution)/shard_map/all_to_all | solution.py:153
  252.7 3.8 %all-to-all-start.4 = ((bf16[16,128,256]{2,1,0:T(8,128)(2,1)}), bf16[16,128,256]{2,1,0:T(8,128)(2,1)S(1)}, u32[]{:S(2)}, u32[]{:S(2)}) async-start(bf16[16,128,256]{2,1,0:T(8,128)(2,1)} %bitcast.30), calls=%async_computation.4 | async-start | bytes 2097152 | tf_op jit(solution)/shard_map/all_to_all | solution.py:156
  256.6 23.8 %all-to-all-done.4 = bf16[16,128,256]{2,1,0:T(8,128)(2,1)S(1)} async-done(((bf16[16,128,256]{2,1,0:T(8,128)(2,1)}), bf16[16,128,256]{2,1,0:T(8,128)(2,1)S(1)}, u32[]{:S(2)}, u32[]{:S(2)}) %all-to-all-start.4) | async-done | bytes 1048608 | tf_op jit(solution)/shard_map/all_to_all | solution.py:156
  282.1 3.1 fusion.1
  285.2 2.5 fusion.27
  287.7 14.1 %all_to_all.56 = bf16[16,64,128]{2,1,0:T(8,128)(2,1)S(1)} all-to-all(bf16[16,64,128]{2,1,0:T(8,128)(2,1)S(1)} %bitcast.146), channel_id=1, replica_groups=mesh['ctx'=16,'tp'=2] {'ctx'}, dimensions={0} | all-to-all | bytes 524288 | tf_op jit(solution)/shard_map/all_to_all | solution.py:165
  (56 shorter events, 29.9 us)
Async XLA Ops:
  7.2 11.2 %copy-start = (bf16[3,1024,128]{2,1,0:T(8,128)(2,1)S(1)}, bf16[3,1024,128]{2,1,0:T(8,128)(2,1)}, u32[]{:S(2)}) copy-start(bf16[3,1024,128]{2,1,0:T(8,128)(2,1)} %param.6) | copy-start | bytes 2359300
  7.2 9.0 %copy-start.2 = (f32[7,3,1024]{2,0,1:T(8,128)S(1)}, f32[7,3,1024]{2,0,1:T(8,128)}, u32[]{:S(2)}) copy-start(f32[7,3,1024]{2,0,1:T(8,128)} %param.7) | copy-start | bytes 258052
  7.2 220.3 %all-gather.2.cloned.1.call-start = ((), (), s32[]{:S(2)}) async-start(), calls=%async_computation.6 | async-start | bytes 13369344 | tf_op jit(solution)/shard_map/all_gather | solution.py:133
  11.4 6.6 %collective-permute-start = (bf16[3,1024,6]{1,2,0:T(8,128)(2,1)S(1)}, bf16[3,1024,6]{1,2,0:T(8,128)(2,1)S(1)}, u32[]{:S(2)}, u32[]{:S(2)}) collective-permute-start(bf16[3,1024,6]{1,2,0:T(8,128)(2,1)S(1)} %copy.98), channel_id=1, source_target_pairs={{0,2},{2,4},{4,6},{6,8},{8,10},{10,12},{12,14},{14,16},{16,18},{18... | collective-permute-start | bytes 110600 | tf_op jit(solution)/shard_map/ppermute | solution.py:17
  40.9 29.0 %all-to-all-start.1 = ((f32[16,64,128]{2,1,0:T(8,128)}), f32[16,64,128]{2,1,0:T(8,128)S(1)}, u32[]{:S(2)}, u32[]{:S(2)}) async-start(f32[16,64,128]{2,1,0:T(8,128)} %bitcast.11), calls=%async_computation.1 | async-start | bytes 1048576 | tf_op jit(solution)/shard_map/all_to_all | solution.py:115
  95.9 28.3 %copy-start.4 = (f32[1024]{0:T(1024)S(1)}, f32[1024]{0:T(1024)}, u32[]{:S(2)}) copy-start(f32[1024]{0:T(1024)} %param.9) | copy-start | bytes 12292
  99.8 127.7 %copy-start.3 = (f32[2048]{0:T(1024)S(1)}, f32[2048]{0:T(1024)}, u32[]{:S(2)}) copy-start(f32[2048]{0:T(1024)} %param.10) | copy-start | bytes 24580
  124.4 112.3 %copy-start.1 = (bf16[1024,128]{1,0:T(8,128)(2,1)}, bf16[1024,128]{1,0:T(8,128)(2,1)S(1)}, u32[]{:S(2)}) copy-start(bf16[1024,128]{1,0:T(8,128)(2,1)S(1)} %fusion.48) | copy-start | bytes 786436
  237.8 13.8 %all-to-all-start.3 = ((bf16[16,64,128]{2,1,0:T(8,128)(2,1)}), bf16[16,64,128]{2,1,0:T(8,128)(2,1)S(1)}, u32[]{:S(2)}, u32[]{:S(2)}) async-start(bf16[16,64,128]{2,1,0:T(8,128)(2,1)} %bitcast.25), calls=%async_computation.3 | async-start | bytes 524288 | tf_op jit(solution)/shard_map/all_to_all | solution.py:153
  252.7 27.7 %all-to-all-start.4 = ((bf16[16,128,256]{2,1,0:T(8,128)(2,1)}), bf16[16,128,256]{2,1,0:T(8,128)(2,1)S(1)}, u32[]{:S(2)}, u32[]{:S(2)}) async-start(bf16[16,128,256]{2,1,0:T(8,128)(2,1)} %bitcast.30), calls=%async_computation.4 | async-start | bytes 2097152 | tf_op jit(solution)/shard_map/all_to_all | solution.py:156
Sparse Core Ops, SparseCore 0:
  10.7 216.6 all-gather.1
where the time goes:
time: 313 us; the launch traced here: 310 us
  waiting for transfers between devices  157 us (50%)
  blocking collectives  56.2 us (18%)
  matrix products  43.5 us (14%)
  starting transfers between devices  16.2 us (5%)
  between operations  14.6 us (5%)
  local copies, waits for them, and re-layouts  12.1 us (4%)
  other arithmetic  10.3 us (3%)
    all_gather x1, waiting for transfers between devices, local(): piece = lax.all_gather(w_qkv, 'ctx', axis=0, tiled=True)  101 us
    dot_general x18, matrix products, contract(): return jnp.einsum(form, data, table, precision=HIGHEST)  30 us
    all_to_all x1, blocking collectives, local(): lax.all_to_all(conv.astype(jnp.bfloat16), 'ctx', split_axis=1, concat_axi...  23.8 us
    all_to_all x1, waiting for transfers between devices, local(): lax.all_to_all(pairs, 'ctx', split_axis=0, concat_axis=0, tiled=True)  23.8 us
    all_to_all x1, waiting for transfers between devices, local(): lax.all_to_all(long_filter, 'ctx', split_axis=0, concat_axis=1, tiled=True)  21 us
    all_to_all x1, blocking collectives, local(): lax.all_to_all(carried, 'ctx', split_axis=0, concat_axis=1, tiled=True)  16 us
    all_to_all x1, blocking collectives, local(): lax.all_to_all(result, 'ctx', split_axis=0, concat_axis=0, tiled=True)  14.1 us
    all_to_all x1, waiting for transfers between devices, local(): lax.all_to_all(queries, 'ctx', split_axis=0, concat_axis=0, tiled=True)  10.1 us
  transfers between devices with their start and end apart: 5, of which 5 were waited for; matrix products, arithmetic and copies ran while one was open for 14% of the time, Pallas kernels for 0%

commit v1 on v0

--- a/solution.py
+++ b/solution.py
@@ -1,8 +1,13 @@
+import functools
 import math
 
 import jax
 import jax.numpy as jnp
+import ml_dtypes
+import numpy as np
 from jax import lax
+from jax.experimental import pallas as pl
+from jax.experimental.pallas import tpu as pltpu
 from jax.sharding import PartitionSpec as P
 
 DH = 128
@@ -169,6 +174,421 @@
     return (mixed, attended)
 
 
+MESH = pl.DeviceIdType.MESH
+F32 = jnp.float32
+BF16 = jnp.bfloat16
+
+
+def split_table(table):
+    high = table.astype(ml_dtypes.bfloat16)
+    low = (table - high.astype(np.float64)).astype(ml_dtypes.bfloat16)
+    return jnp.asarray(high), jnp.asarray(low)
+
+
+def packed_tables(tok):
+    full = 2 * tok
+    pos = np.arange(tok)[:, None]
+    freq = np.arange(tok)[None, :]
+    angle = 2.0 * np.pi * ((pos * freq) % full) / full
+    imag = -np.sin(angle)
+    imag[:, 0] = (-1.0) ** np.arange(tok)
+    forward = np.concatenate([np.cos(angle), imag], axis=1)
+    out = np.arange(full)[None, :]
+    freq = np.arange(tok)[:, None]
+    angle = 2.0 * np.pi * ((out * freq) % full) / full
+    real = 2.0 * np.cos(angle)
+    real[0] = 1.0
+    imag = -2.0 * np.sin(angle)
+    imag[0] = (-1.0) ** np.arange(full)
+    backward = np.concatenate([real, imag], axis=0) / full
+    return split_table(forward) + split_table(backward)
+
+
+def hyena_kernel(
+    dims,
+    feats,
+    filt,
+    wts,
+    coef,
+    fwd_hi,
+    fwd_lo,
+    inv_hi,
+    inv_lo,
+    gathered,
+    w_all,
+    feat_all,
+    filt_all,
+    short0,
+    carried,
+    spec_x,
+    spec_f,
+    mixed,
+    local_sem,
+    feat_send,
+    feat_recv,
+    filt_send,
+    filt_recv,
+    w_send,
+    w_recv,
+    wx_send,
+    wx_recv,
+    x_send,
+    x_recv,
+    z_send,
+    z_recv,
+    y_send,
+    y_recv,
+    s_send,
+    s_recv,
+):
+    ranks, nz, taps = dims
+    me = lax.axis_index("ctx")
+    core = lax.axis_index("tp")
+    x = me % 2
+    pair = me // 2
+    y = pair % 2
+    z = pair // 2
+    width = filt_all.shape[1]
+    tok = filt_all.shape[2]
+    pairs = ranks // 2
+
+    barrier = pltpu.get_barrier_semaphore()
+
+    def greet(d, _):
+        pl.semaphore_signal(
+            barrier, inc=1, device_id=((me + d) % ranks, core), device_id_type=MESH
+        )
+        return 0
+
+    lax.fori_loop(1, ranks, greet, 0)
+    pl.semaphore_signal(barrier, inc=1, device_id=(me, 1 - core), device_id_type=MESH)
+    pl.semaphore_wait(barrier, ranks)
+
+    def remote(src, dst, send, recv, ctx, tp):
+        return pltpu.make_async_remote_copy(
+            src_ref=src, dst_ref=dst, send_sem=send, recv_sem=recv,
+            device_id=(ctx, tp), device_id_type=MESH,
+        )
+
+    def feat_copy(d):
+        to = (me + d) % ranks
+        return remote(
+            feats.at[:, pl.ds(to * width, width)], feat_all.at[me],
+            feat_send.at[d], feat_recv.at[d], to, core,
+        )
+
+    def filt_copy(d):
+        to = (me + d) % ranks
+        return remote(
+            filt.at[pl.ds(to * width, width)], filt_all.at[me],
+            filt_send.at[d], filt_recv.at[d], to, core,
+        )
+
+    def w_copy(d):
+        to = (pair + d) % pairs
+        return remote(
+            wts.at[to], w_all.at[pair, x], w_send.at[d], w_recv.at[d], to * 2 + x, core
+        )
+
+    own = [
+        pltpu.make_async_copy(
+            feats.at[:, pl.ds(me * width, width)], feat_all.at[me], local_sem.at[0]
+        ),
+        pltpu.make_async_copy(filt.at[pl.ds(me * width, width)], filt_all.at[me], local_sem.at[1]),
+        pltpu.make_async_copy(wts.at[pair], w_all.at[pair, x], local_sem.at[2]),
+    ]
+    for copy in own:
+        copy.start()
+    for d in range(1, ranks):
+        feat_copy(d).start()
+    for d in range(1, ranks):
+        filt_copy(d).start()
+    for d in range(1, pairs):
+        w_copy(d).start()
+    own[0].wait()
+    own[1].wait()
+    for d in range(1, ranks):
+        feat_copy(d).wait_recv()
+
+    lane = lax.broadcasted_iota(jnp.int32, (width, tok), 1)
+    first = lane == 0
+
+    def short_block(b, _):
+        before = jnp.maximum(b - 1, 0)
+        live = jnp.where(b > 0, 1.0, 0.0).astype(F32)
+        sums = []
+        for i in range(3):
+            now = feat_all[b, i].astype(F32)
+            past = feat_all[before, i].astype(F32) * live
+            total = coef[:, i : i + 1] * now
+            for lag in range(1, taps):
+                moved = jnp.where(
+                    lane < lag, pltpu.roll(past, lag, 1), pltpu.roll(now, lag, 1)
+                )
+                total = total + coef[:, lag * 3 + i : lag * 3 + i + 1] * moved
+            sums.append(total)
+        short0[b] = sums[0]
+        held = (sums[1] * sums[2]).astype(BF16)
+        carried[b] = held
+        spec_x[b] = jnp.dot(held, fwd_hi[...], preferred_element_type=F32) + jnp.dot(
+            held, fwd_lo[...], preferred_element_type=F32
+        )
+        return 0
+
+    lax.fori_loop(0, ranks, short_block, 0)
+    for d in range(1, ranks):
+        filt_copy(d).wait_recv()
+
+    def filter_block(b, _):
+        lags = filt_all[b]
+        spec = jnp.dot(lags, fwd_hi[...], preferred_element_type=F32) + jnp.dot(
+            lags, fwd_lo[...], preferred_element_type=F32
+        )
+        real = spec[:, :tok]
+        imag = spec[:, tok:]
+        spec_f[b, 0] = real
+        spec_f[b, 1] = jnp.where(first, 0.0, imag)
+        spec_f[b, 2] = jnp.where(first, imag, real)
+        return 0
+
+    lax.fori_loop(0, ranks, filter_block, 0)
+
+    def block(m, tail):
+        def term(d, acc):
+            real, imag = acc
+            xr = spec_x[m - d, :, :tok]
+            xi = spec_x[m - d, :, tok:]
+            f_re = spec_f[d, 0]
+            f_im = spec_f[d, 1]
+            f_ny = spec_f[d, 2]
+            return (real + (xr * f_re - xi * f_im), imag + (xr * f_im + xi * f_ny))
+
+        zero = jnp.zeros((width, tok), F32)
+        real, imag = lax.fori_loop(0, m + 1, term, (zero, zero))
+        spec = jnp.concatenate([real, imag], axis=1)
+        high = spec.astype(BF16)
+        low = (spec - high.astype(F32)).astype(BF16)
+        wave = (
+            jnp.dot(high, inv_hi[...], preferred_element_type=F32)
+            + jnp.dot(low, inv_hi[...], preferred_element_type=F32)
+            + jnp.dot(high, inv_lo[...], preferred_element_type=F32)
+        )
+        long_out = (wave[:, :tok] + tail).astype(BF16).astype(F32)
+        skip = coef[:, 3 * taps : 3 * taps + 1]
+        value = short0[m] * (long_out + skip * carried[m].astype(F32))
+        mixed[m % 2, :, pl.ds(pl.multiple_of((m // 2) * tok, tok), tok)] = value.astype(BF16)
+        return wave[:, tok:]
+
+    lax.fori_loop(0, ranks, block, jnp.zeros((width, tok), F32))
+
+    keep = pltpu.make_async_copy(mixed.at[x], gathered.at[core, pair, x], local_sem.at[3])
+    keep.start()
+    swap = remote(
+        mixed.at[1 - x], gathered.at[core, pair, x], x_send.at[0], x_recv.at[0],
+        pair * 2 + 1 - x, core,
+    )
+    swap.start()
+    keep.wait()
+    swap.wait_recv()
+
+    def chunk(p):
+        return gathered.at[core, p]
+
+    def z_copy(d):
+        to = (z + d) % nz
+        return remote(
+            chunk(pair), chunk(pair), z_send.at[d], z_recv.at[d], to * 4 + y * 2 + x, core
+        )
+
+    def y_copy(d):
+        p = ((z - d + nz) % nz) * 2 + y
+        return remote(
+            chunk(p), chunk(p), y_send.at[d], y_recv.at[d], z * 4 + (1 - y) * 2 + x, core
+        )
+
+    def s_copy(d, side):
+        p = ((z - d + nz) % nz) * 2 + jnp.where(side == 0, y, 1 - y)
+        return remote(
+            chunk(p), chunk(p), s_send.at[side * nz + d], s_recv.at[side * nz + d], me, 1 - core
+        )
+
+    y_copy(0).start()
+    for d in range(1, nz):
+        z_copy(d).start()
+    s_copy(0, 0).start()
+
+    own[2].wait()
+    for d in range(1, pairs):
+        w_copy(d).wait_recv()
+    w_swap = remote(
+        w_all.at[:, x], w_all.at[:, x], wx_send.at[0], wx_recv.at[0], pair * 2 + 1 - x, core
+    )
+    w_swap.start()
+
+    for d in range(1, nz):
+        z_copy(d).wait_recv()
+        y_copy(d).start()
+        s_copy(d, 0).start()
+    for d in range(nz):
+        y_copy(d).wait_recv()
+        s_copy(d, 1).start()
+    for d in range(nz):
+        s_copy(d, 0).wait_recv()
+        s_copy(d, 1).wait_recv()
+    w_swap.wait()
+    for d in range(1, ranks):
+        feat_copy(d).wait_send()
+        filt_copy(d).wait_send()
+    for d in range(1, pairs):
+        w_copy(d).wait_send()
+    swap.wait_send()
+    for d in range(1, nz):
+        z_copy(d).wait_send()
+    for d in range(nz):
+        y_copy(d).wait_send()
+        s_copy(d, 0).wait_send()
+        s_copy(d, 1).wait_send()
+
+
+def hyena(features, filt, wts, coef, nz, taps):
+    ranks = features.shape[1] // coef.shape[0]
+    width = coef.shape[0]
+    tok = features.shape[2]
+    pairs = ranks // 2
+    rows, columns = wts.shape[1:]
+    tables = packed_tables(tok)
+    vmem = pl.BlockSpec(memory_space=pltpu.VMEM)
+    hbm = pl.BlockSpec(memory_space=pl.ANY)
+    dma = pltpu.SemaphoreType.DMA
+    return pl.pallas_call(
+        functools.partial(hyena_kernel, (ranks, nz, taps)),
+        out_shape=(
+            jax.ShapeDtypeStruct((2, pairs, 2, width, pairs * tok), BF16),
+            jax.ShapeDtypeStruct((pairs, 2, rows, columns), BF16),
+        ),
+        in_specs=[hbm, hbm, hbm] + [vmem] * 5,
+        out_specs=(hbm, hbm),
+        scratch_shapes=[
+            pltpu.VMEM((ranks, 3, width, tok), BF16),
+            pltpu.VMEM((ranks, width, tok), BF16),
+            pltpu.VMEM((ranks, width, tok), F32),
+            pltpu.VMEM((ranks, width, tok), BF16),
+            pltpu.VMEM((ranks, width, 2 * tok), F32),
+            pltpu.VMEM((ranks, 3, width, tok), F32),
+            pltpu.VMEM((2, width, pairs * tok), BF16),
+            dma((4,)),
+            dma((ranks,)),
+            dma((ranks,)),
+            dma((ranks,)),
+            dma((ranks,)),
+            dma((pairs,)),
+            dma((pairs,)),
+            dma((1,)),
+            dma((1,)),
+            dma((1,)),
+            dma((1,)),
+            dma((nz,)),
+            dma((nz,)),
+            dma((nz,)),
+            dma((nz,)),
+            dma((2 * nz,)),
+            dma((2 * nz,)),
+        ],
+        compiler_params=pltpu.CompilerParams(
+            collective_id=0, has_side_effects=True, vmem_limit_bytes=32 * 2**20
+        ),
+    )(features, filt, wts, coef, *tables)
+
+
+def return_kernel(pairs, result, out, local_sem, send, recv):
+    me = lax.axis_index("ctx")
+    core = lax.axis_index("tp")
+    x = me % 2
+    pair = me // 2
+    barrier = pltpu.get_barrier_semaphore()
+    for d in range(1, pairs):
+        to = (pair + d) % pairs
+        pl.semaphore_signal(barrier, inc=1, device_id=(to * 2 + x, core), device_id_type=MESH)
+    pl.semaphore_wait(barrier, pairs - 1)
+    own = pltpu.make_async_copy(result.at[pair], out.at[pair], local_sem)
+    own.start()
+
+    def copy(d):
+        to = (pair + d) % pairs
+        return pltpu.make_async_remote_copy(
+            src_ref=result.at[to], dst_ref=out.at[pair], send_sem=send.at[d],
+            recv_sem=recv.at[d], device_id=(to * 2 + x, core), device_id_type=MESH,
+        )
+
+    for d in range(1, pairs):
+        copy(d).start()
+    own.wait()
+    for d in range(1, pairs):
+        copy(d).wait()
+
+
+def give_back(result):
+    pairs = result.shape[0]
+    hbm = pl.BlockSpec(memory_space=pltpu.VMEM)
+    return pl.pallas_call(
+        functools.partial(return_kernel, pairs),
+        out_shape=jax.ShapeDtypeStruct(result.shape, result.dtype),
+        in_specs=[hbm],
+        out_specs=hbm,
+        scratch_shapes=[
+            pltpu.SemaphoreType.DMA,
+            pltpu.SemaphoreType.DMA((pairs,)),
+            pltpu.SemaphoreType.DMA((pairs,)),
+        ],
+        compiler_params=pltpu.CompilerParams(collective_id=1, has_side_effects=True),
+    )(result)
+
+
+def local_pairs(features, short_taps, long_filter, skip, norm_gain, w_qkv):
+    ranks = lax.axis_size("ctx")
+    pairs = ranks // 2
+    me = lax.axis_index("ctx")
+    core = lax.axis_index("tp")
+    x = me % 2
+    taps = short_taps.shape[0]
+    tok = features.shape[2]
+    width = features.shape[1] // ranks
+    coef = jnp.concatenate([short_taps.reshape(taps * 3, -1), skip[None]], axis=0)
+    coef = lax.dynamic_slice_in_dim(coef, me * width, width, 1).T
+    rows = w_qkv.shape[0]
+    wts = jnp.transpose(w_qkv.reshape(rows, 3, pairs, DH), (2, 0, 1, 3)).reshape(
+        pairs, rows, 3 * DH
+    )
+    gathered, w_all = hyena(
+        features, long_filter.astype(BF16), wts, coef, ranks // 4, taps
+    )
+    channels = norm_gain.shape[0]
+    whole = gathered.reshape(channels, pairs * tok)
+    half = lax.dynamic_slice(
+        whole, (core * (channels // 2), (me // 2) * tok), (channels // 2, tok)
+    )
+    whole_f = whole.astype(F32)
+    inverse = lax.rsqrt(jnp.mean(whole_f * whole_f, axis=0, keepdims=True) + 1e-06)
+    normed = (whole_f * inverse * norm_gain[:, None]).astype(BF16)
+    projected = lax.dot_general(
+        normed, w_all.reshape(channels, 3 * DH), (((0,), (0,)), ((), ())),
+        preferred_element_type=F32,
+    ).astype(BF16)
+    mine = projected[:, DH:]
+    other = lax.ppermute(mine, "ctx", [(i, i ^ 1) for i in range(ranks)])
+    mine = mine.reshape(pairs, 1, tok, 2 * DH)
+    other = other.reshape(pairs, 1, tok, 2 * DH)
+    even = jnp.where(x == 0, mine, other)
+    odd = jnp.where(x == 0, other, mine)
+    keyvals = jnp.concatenate([even, odd], axis=1).reshape(ranks * tok, 2 * DH)
+    source = jnp.arange(pairs * tok, dtype=jnp.int32)
+    query_pos = (source // tok * 2 + x) * tok + source % tok
+    result = attend_rows(projected[:, :DH], query_pos, keyvals, 1, ranks * tok)
+    back = give_back(result.astype(BF16).reshape(pairs, tok, DH))
+    attended = jnp.transpose(back, (1, 0, 2)).reshape(tok, pairs * DH)
+    return (half, attended)
+
+
 def solution(mesh):
     in_specs = (
         P(None, "tp", "ctx"),
@@ -179,4 +599,13 @@
         P("ctx", None, "tp"),
     )
     out_specs = (P("tp", "ctx"), P("ctx", "tp"))
-    return jax.shard_map(local, mesh=mesh, in_specs=in_specs, out_specs=out_specs, check_vma=False)
+
+    def whole(features, short_taps, long_filter, skip, norm_gain, w_qkv):
+        heads = w_qkv.shape[2] // mesh.shape["tp"] // DH
+        paired = mesh.shape["ctx"] == 16 and heads == 8
+        body = local_pairs if paired else local
+        return jax.shard_map(
+            body, mesh=mesh, in_specs=in_specs, out_specs=out_specs, check_vma=False
+        )(features, short_taps, long_filter, skip, norm_gain, w_qkv)
+
+    return whole

time: 313 us -> 147 us (0.47)
  waiting for transfers between devices: 157 us -> 12.3 us
  Pallas kernels: 0 us -> 106 us
  blocking collectives: 56.2 us -> 0 us
  matrix products: 43.5 us -> 7.75 us
  starting transfers between devices: 16.2 us -> 0.41 us
  between operations: 14.6 us -> 0.77 us
  other arithmetic: 10.3 us -> 7.12 us
    pallas_call x0 -> x2, Pallas kernels: none -> 106 us  [the longest x1 80.3 us: hyena(): pl.pallas_call(functools.partial(hyena_kernel, (ranks, nz, taps)), out_sh...]
    all_gather x1 -> x0, waiting for transfers between devices: 101 us -> none  [local(): piece = lax.all_gather(w_qkv, 'ctx', axis=0, tiled=True)]
    all_to_all x3 -> x0, waiting for transfers between devices: 54.9 us -> none  [the longest x1 23.8 us: local(): lax.all_to_all(pairs, 'ctx', split_axis=0, concat_axis=0, tiled=True)]
    all_to_all x3 -> x0, blocking collectives: 54 us -> none  [the longest x1 23.8 us: local(): lax.all_to_all(conv.astype(jnp.bfloat16), 'ctx', split_axis=1, concat_axi...]
    dot_general x19 -> x1, matrix products: 39.3 us -> 2.4 us  [local_pairs(): lax.dot_general(normed, w_all.reshape(channels, 3 * DH), (((0,), (0,)), (...]
    all_to_all x3 -> x0, starting transfers between devices: 11.3 us -> none  [the longest x1 3.96 us: local(): lax.all_to_all(long_filter, 'ctx', split_axis=0, concat_axis=1, tiled=True)]
    ppermute x1, waiting for transfers between devices: 1.58 us -> 12.3 us  [local_pairs(): other = lax.ppermute(mine, 'ctx', [(i, i ^ 1) for i in range(ranks)])]
    add x2 -> x1, other arithmetic: 5.89 us -> 0.01 us  [local_pairs(): query_pos = (source // tok * 2 + x) * tok + source % tok]
  transfers between devices with their start and end apart: 5 -> 1, of which waited for: 5 -> 1; matrix products, arithmetic and copies ran while one was open for 14% -> 1% of each run, Pallas kernels for 0% -> 0%
where the time goes in v1:
time: 147 us
  Pallas kernels  106 us (72%)
  waiting for transfers between devices  12.3 us (8%)
  local copies, waits for them, and re-layouts  12.1 us (8%)
  matrix products  7.75 us (5%)
  other arithmetic  7.12 us (5%)
    pallas_call x1, Pallas kernels, hyena(): pl.pallas_call(functools.partial(hyena_kernel, (ranks, nz, taps)), out_sh...  80.3 us
    pallas_call x1, Pallas kernels, give_back(): pl.pallas_call(functools.partial(return_kernel, pairs), out_shape=jax.Sha...  26.1 us
    ppermute x1, waiting for transfers between devices, local_pairs(): other = lax.ppermute(mine, 'ctx', [(i, i ^ 1) for i in range(ranks)])  12.3 us
    unnamed x16, local copies, waits for them, and re-layouts  8.03 us
    dot_general x1, matrix products, step(): jnp.dot(expo.astype(jnp.bfloat16), vals, preferred_element_type=jnp.float32)  3.61 us
    reduce_sum x1, other arithmetic, step(): total = total * factor + jnp.sum(expo, axis=1)  3.07 us
  transfers between devices with their start and end apart: 1, of which 1 were waited for; matrix products, arithmetic and copies ran while one was open for 1% of the time, Pallas kernels for 0%

profile of v1, /device:TPU:0, one launch (start us, length us, event | category | flops | bytes accessed | tf_op | source)
XLA Modules:
  0.0 146.8 jit_solution(17273195381192702338)
XLA Ops:
  0.6 0.8 mul.86
  1.4 1.0 copy.34
  2.4 0.7 fusion.21
  3.3 1.1 convert_element_type.24.filt
  4.3 1.5 %copy.32 = bf16[128,3,1024]{0,2,1:T(8,128)(2,1)S(1)} copy(bf16[128,3,1024]{2,0,1:T(8,128)(2,1)} %param.15) | data formatting | bytes 1572864 | tf_op args[5]
  5.9 0.4 copy.36.wts
  6.3 1.1 copy-done.1
  7.4 0.9 copy-done.2
  8.3 0.9 copy-done.3
  9.2 0.8 copy-done.4
  10.1 0.8 copy-done.5
  10.9 80.3 %shard_map.113 = (bf16[2,8,2,64,1024]{4,3,2,1,0:T(8,128)(2,1)S(1)}, bf16[8,2,128,384]{3,2,1,0:T(8,128)(2,1)S(1)}) custom-call(bf16[3,1024,128]{2,1,0:T(8,128)(2,1)S(1)} %copy-done.1, bf16[1024,128]{1,0:T(8,128)(2,1)S(1)} %convert_element_type.24.filt, bf16[8,128,384]{2,1,0:T(8,128)(2,1)S(1)} %copy.36.wts, f32[64,22]{1,0:T(8,128)S(1)} %bitcast.22, ...), custom_call_target="tpu_custom_call" | custom-call | tf_op jit(solution)/shard_map/pallas_call | solution.py:463
  91.2 0.9 fusion
  92.1 1.1 fusion.2
  93.2 2.4 %convolution_convert_fusion = bf16[1024,384]{1,0:T(8,128)(2,1)S(1)} fusion(bf16[2048,1024]{1,0:T(8,128)(2,1)S(1)} %bitcast.24, bf16[2048,384]{1,0:T(8,128)(2,1)S(1)} %bitcast.23), kind=kOutput, calls=%fused_computation.12 | convolution fusion | flops 1611005952 | bytes 6553600 | tf_op jit(solution)/shard_map/dot_general | solution.py:573
  95.7 0.4 collective-permute-start
  96.1 1.7 %dynamic_slice.9 = bf16[1024,128]{1,0:T(8,128)(2,1)} dynamic-slice(bf16[2048,1024]{1,0:T(8,128)(2,1)} %bitcast.21, s32[]{:T(128)S(6)} %select_n.85, s32[]{:T(128)S(6)} %select_n.87), dynamic_slice_sizes={1024,128} | dynamic-slice | bytes 524292 | tf_op jit(solution)/shard_map/dynamic_slice | solution.py:567
  97.8 12.3 %collective-permute-done = bf16[1024,256]{1,0:T(8,128)(2,1)S(1)} collective-permute-done((bf16[1024,256]{1,0:T(8,128)(2,1)S(1)}, bf16[1024,256]{1,0:T(8,128)(2,1)S(1)}, u32[]{:S(2)}, u32[]{:S(2)}) %collective-permute-start) | collective-permute-done | bytes 524320 | tf_op jit(solution)/shard_map/ppermute | solution.py:578
  110.2 1.7 %fusion.3 = (f32[1024]{0:T(1024)S(1)}, f32[1024,2048]{1,0:T(8,128)S(1)}) fusion(s32[1024]{0:T(1024)S(1)} %fusion.31, bf16[2048,256]{1,0:T(8,128)(2,1)S(1)} %bitcast.29, bf16[1024,384]{1,0:T(8,128)(2,1)S(1)} %convolution_convert_fusion), kind=kOutput, calls=%fused_computation.8 | convolution fusion | flops 545258496 | bytes 9183232 | tf_op jit(solution)/shard_map/while/body/eval_jaxpr/dot_general | solution.py:84
  112.0 3.1 %fusion.4 = f32[1024]{0:T(1024)S(1)} fusion(f32[1024,2048]{1,0:T(8,128)S(1)} %get-tuple-element.41, f32[1024]{0:T(1024)S(1)} %broadcast_maximum_fusion, s32[1024]{0:T(1024)S(1)} %fusion.31), kind=kLoop, calls=%fused_computation.9 | loop fusion | flops 12581888 | bytes 8400896 | tf_op jit(solution)/shard_map/while/body/eval_jaxpr/reduce_sum | solution.py:95
  115.1 3.6 %fusion.14 = bf16[1024,128]{1,0:T(8,128)(2,1)} fusion(f32[1024,2048]{1,0:T(8,128)S(1)} %get-tuple-element.41, f32[1024]{0:T(1024)S(1)} %broadcast_maximum_fusion, s32[1024]{0:T(1024)S(1)} %fusion.31, bf16[2048,256]{1,0:T(8,128)(2,1)S(1)} %bitcast.30, f32[1024]{0:T(1024)S(1)} %get-tuple-element.39, f32[1024]{0:T(1024)S(1)} %get-tuple-element.38), kind=kOutput, calls=%fused_computation.16 | convolution fusion | flops 549847040 | bytes 9191424 | tf_op jit(solution)/shard_map/while/body/eval_jaxpr/dot_general | solution.py:96
  118.7 26.1 %shard_map.114 = bf16[8,128,128]{2,1,0:T(8,128)(2,1)} custom-call(bf16[8,128,128]{2,1,0:T(8,128)(2,1)} %bitcast.33), custom_call_target="tpu_custom_call" | custom-call | tf_op jit(solution)/shard_map/pallas_call | solution.py:533
  144.8 1.1 copy.39
  145.9 0.9 copy.40
  (17 shorter events, 0.5 us)
Async XLA Ops:
  6.3 1.1 copy-start.1
  7.4 0.9 copy-start.2
  8.3 0.9 copy-start.3
  9.2 0.8 copy-start.4
  10.1 0.8 copy-start.5
  91.2 4.5 %copy-start = (bf16[2,8,2,64,1024]{4,3,2,1,0:T(8,128)(2,1)}, bf16[2,8,2,64,1024]{4,3,2,1,0:T(8,128)(2,1)S(1)}, u32[]{:S(2)}) copy-start(bf16[2,8,2,64,1024]{4,3,2,1,0:T(8,128)(2,1)S(1)} %get-tuple-element.20) | copy-start | bytes 12582916
  95.7 14.3 %collective-permute-start = (bf16[1024,256]{1,0:T(8,128)(2,1)S(1)}, bf16[1024,256]{1,0:T(8,128)(2,1)S(1)}, u32[]{:S(2)}, u32[]{:S(2)}) collective-permute-start(bf16[1024,256]{1,0:T(8,128)(2,1)S(1)} %slice.19), channel_id=1, source_target_pairs={{0,2},{2,0},{4,6},{6,4},{8,10},{10,8},{12,14},{14,12},{16,18},{18,... | collective-permute-start | bytes 1572872 | tf_op jit(solution)/shard_map/ppermute | solution.py:578

commit v2 on v1

--- a/solution.py
+++ b/solution.py
@@ -207,15 +207,24 @@
 def hyena_kernel(
     dims,
     feats,
+    filt_in,
+    w_in,
+    coef_in,
+    fwd_hi_in,
+    fwd_lo_in,
+    inv_hi_in,
+    inv_lo_in,
+    gathered,
+    w_all,
+    filt_wide,
     filt,
+    w_raw,
     wts,
     coef,
     fwd_hi,
     fwd_lo,
     inv_hi,
     inv_lo,
-    gathered,
-    w_all,
     feat_all,
     filt_all,
     short0,
@@ -290,6 +299,24 @@
             wts.at[to], w_all.at[pair, x], w_send.at[d], w_recv.at[d], to * 2 + x, core
         )
 
+    loads = [
+        pltpu.make_async_copy(src, dst, local_sem.at[4 + i])
+        for i, (src, dst) in enumerate(
+            (
+                (filt_in, filt_wide),
+                (w_in, w_raw),
+                (coef_in, coef),
+                (fwd_hi_in, fwd_hi),
+                (fwd_lo_in, fwd_lo),
+                (inv_hi_in, inv_hi),
+                (inv_lo_in, inv_lo),
+            )
+        )
+    ]
+    for d in range(1, ranks):
+        feat_copy(d).start()
+    for load in loads:
+        load.start()
     own = [
         pltpu.make_async_copy(
             feats.at[:, pl.ds(me * width, width)], feat_all.at[me], local_sem.at[0]
@@ -297,18 +324,25 @@
         pltpu.make_async_copy(filt.at[pl.ds(me * width, width)], filt_all.at[me], local_sem.at[1]),
         pltpu.make_async_copy(wts.at[pair], w_all.at[pair, x], local_sem.at[2]),
     ]
-    for copy in own:
-        copy.start()
-    for d in range(1, ranks):
-        feat_copy(d).start()
+    own[0].start()
+    loads[0].wait()
+    filt[...] = filt_wide[...].astype(BF16)
+    own[1].start()
     for d in range(1, ranks):
         filt_copy(d).start()
-    for d in range(1, pairs):
-        w_copy(d).start()
+    loads[1].wait()
+    for i in range(3):
+        for h in range(pairs):
+            wts[h, :, i * DH : (i + 1) * DH] = w_raw[:, i, h * DH : (h + 1) * DH]
+    own[2].start()
+    for load in loads[2:]:
+        load.wait()
     own[0].wait()
     own[1].wait()
     for d in range(1, ranks):
         feat_copy(d).wait_recv()
+    for d in range(1, pairs):
+        w_copy(d).start()
 
     lane = lax.broadcasted_iota(jnp.int32, (width, tok), 1)
     first = lane == 0
@@ -450,14 +484,14 @@
         s_copy(d, 1).wait_send()
 
 
-def hyena(features, filt, wts, coef, nz, taps):
+def hyena(features, filt, w_qkv, coef, nz, taps):
     ranks = features.shape[1] // coef.shape[0]
     width = coef.shape[0]
     tok = features.shape[2]
     pairs = ranks // 2
-    rows, columns = wts.shape[1:]
+    rows = w_qkv.shape[0]
+    columns = 3 * DH
     tables = packed_tables(tok)
-    vmem = pl.BlockSpec(memory_space=pltpu.VMEM)
     hbm = pl.BlockSpec(memory_space=pl.ANY)
     dma = pltpu.SemaphoreType.DMA
     return pl.pallas_call(
@@ -466,9 +500,17 @@
             jax.ShapeDtypeStruct((2, pairs, 2, width, pairs * tok), BF16),
             jax.ShapeDtypeStruct((pairs, 2, rows, columns), BF16),
         ),
-        in_specs=[hbm, hbm, hbm] + [vmem] * 5,
+        in_specs=[hbm] * 8,
         out_specs=(hbm, hbm),
         scratch_shapes=[
+            pltpu.VMEM(filt.shape, F32),
+            pltpu.VMEM(filt.shape, BF16),
+            pltpu.VMEM(w_qkv.shape, BF16),
+            pltpu.VMEM((pairs, rows, columns), BF16),
+            pltpu.VMEM(coef.shape, F32),
+        ]
+        + [pltpu.VMEM(table.shape, BF16) for table in tables]
+        + [
             pltpu.VMEM((ranks, 3, width, tok), BF16),
             pltpu.VMEM((ranks, width, tok), BF16),
             pltpu.VMEM((ranks, width, tok), F32),
@@ -476,7 +518,7 @@
             pltpu.VMEM((ranks, width, 2 * tok), F32),
             pltpu.VMEM((ranks, 3, width, tok), F32),
             pltpu.VMEM((2, width, pairs * tok), BF16),
-            dma((4,)),
+            dma((11,)),
             dma((ranks,)),
             dma((ranks,)),
             dma((ranks,)),
@@ -497,51 +539,137 @@
         compiler_params=pltpu.CompilerParams(
             collective_id=0, has_side_effects=True, vmem_limit_bytes=32 * 2**20
         ),
-    )(features, filt, wts, coef, *tables)
-
-
-def return_kernel(pairs, result, out, local_sem, send, recv):
+    )(features, filt, w_qkv, coef, *tables)
+
+
+def attend_kernel(
+    pairs, tok, proj, out, other, top, total, accum, result,
+    local_sem, kv_send, kv_recv, send, recv,
+):
     me = lax.axis_index("ctx")
     core = lax.axis_index("tp")
     x = me % 2
     pair = me // 2
+    parts = kv_send.shape[0]
+    rows = pairs * tok // parts
+    scale = DH ** (-0.5)
+
     barrier = pltpu.get_barrier_semaphore()
     for d in range(1, pairs):
         to = (pair + d) % pairs
         pl.semaphore_signal(barrier, inc=1, device_id=(to * 2 + x, core), device_id_type=MESH)
-    pl.semaphore_wait(barrier, pairs - 1)
-    own = pltpu.make_async_copy(result.at[pair], out.at[pair], local_sem)
+    pl.semaphore_signal(
+        barrier, inc=1, device_id=(pair * 2 + 1 - x, core), device_id_type=MESH
+    )
+    pl.semaphore_wait(barrier, pairs)
+
+    def kv_copy(c):
+        return pltpu.make_async_remote_copy(
+            src_ref=proj.at[pl.ds(c * rows, rows), pl.ds(DH, 2 * DH)],
+            dst_ref=other.at[pl.ds(c * rows, rows)],
+            send_sem=kv_send.at[c], recv_sem=kv_recv.at[c],
+            device_id=(pair * 2 + 1 - x, core), device_id_type=MESH,
+        )
+
+    for c in range(parts):
+        kv_copy(c).start()
+
+    def dot_t(a, b):
+        return lax.dot_general(a, b, (((1,), (1,)), ((), ())), preferred_element_type=F32)
+
+    for j in range(pairs):
+        here = pl.ds(j * tok, tok)
+        count = (j + 1) * tok
+        scores = dot_t(proj[here, :DH], proj[:count, DH : 2 * DH]) * scale
+        col = lax.broadcasted_iota(jnp.int32, (tok, count), 1)
+        row = lax.broadcasted_iota(jnp.int32, (tok, count), 0)
+        scores = jnp.where(col <= row + j * tok, scores, -1e30)
+        peak = jnp.max(scores, axis=1, keepdims=True)
+        expo = jnp.exp(scores - peak)
+        top[here] = jnp.broadcast_to(peak, (tok, DH))
+        total[here] = jnp.broadcast_to(jnp.sum(expo, axis=1, keepdims=True), (tok, DH))
+        accum[here] = jnp.dot(
+            expo.astype(BF16), proj[:count, 2 * DH :], preferred_element_type=F32
+        )
+
+    def back_copy(j):
+        return pltpu.make_async_remote_copy(
+            src_ref=result.at[j], dst_ref=out.at[:, pl.ds(pl.multiple_of(pair * DH, DH), DH)],
+            send_sem=send.at[j], recv_sem=recv.at[pair],
+            device_id=(j * 2 + x, core), device_id_type=MESH,
+        )
+
+    for j in range(pairs):
+        here = pl.ds(j * tok, tok)
+        count = (j + 1) * tok
+        if j * tok % rows == 0:
+            kv_copy(j * tok // rows).wait_recv()
+        scores = dot_t(proj[here, :DH], other[:count, :DH]) * scale
+        col = lax.broadcasted_iota(jnp.int32, (tok, count), 1)
+        scores = jnp.where(col < (j + x) * tok, scores, -1e30)
+        peak = top[here]
+        new_peak = jnp.maximum(peak, jnp.max(scores, axis=1, keepdims=True))
+        factor = jnp.exp(peak - new_peak)
+        expo = jnp.exp(scores - new_peak[:, :1])
+        summed = total[here] * factor + jnp.sum(expo, axis=1, keepdims=True)
+        value = accum[here] * factor + jnp.dot(
+            expo.astype(BF16), other[:count, DH:], preferred_element_type=F32
+        )
+        result[j] = (value / summed).astype(BF16)
+
+        @pl.when(j != pair)
+        def _():
+            back_copy(j).start()
+
+    own = pltpu.make_async_copy(
+        result.at[pair], out.at[:, pl.ds(pl.multiple_of(pair * DH, DH), DH)], local_sem
+    )
     own.start()
-
-    def copy(d):
-        to = (pair + d) % pairs
-        return pltpu.make_async_remote_copy(
-            src_ref=result.at[to], dst_ref=out.at[pair], send_sem=send.at[d],
-            recv_sem=recv.at[d], device_id=(to * 2 + x, core), device_id_type=MESH,
-        )
+    own.wait()
+    for c in range(parts):
+        kv_copy(c).wait_send()
+    for j in range(pairs):
+
+        @pl.when(j != pair)
+        def _():
+            back_copy(j).wait_send()
 
     for d in range(1, pairs):
-        copy(d).start()
-    own.wait()
-    for d in range(1, pairs):
-        copy(d).wait()
-
-
-def give_back(result):
-    pairs = result.shape[0]
-    hbm = pl.BlockSpec(memory_space=pltpu.VMEM)
+        frm = (pair + d) % pairs
+        pltpu.make_async_remote_copy(
+            src_ref=result.at[frm],
+            dst_ref=out.at[:, pl.ds(pl.multiple_of(frm * DH, DH), DH)],
+            send_sem=send.at[frm], recv_sem=recv.at[frm],
+            device_id=(frm * 2 + x, core), device_id_type=MESH,
+        ).wait_recv()
+
+
+def attend(projected, pairs, tok):
+    vmem = pl.BlockSpec(memory_space=pltpu.VMEM)
+    dma = pltpu.SemaphoreType.DMA
+    rows = pairs * tok
+    parts = 4
     return pl.pallas_call(
-        functools.partial(return_kernel, pairs),
-        out_shape=jax.ShapeDtypeStruct(result.shape, result.dtype),
-        in_specs=[hbm],
-        out_specs=hbm,
+        functools.partial(attend_kernel, pairs, tok),
+        out_shape=jax.ShapeDtypeStruct((tok, pairs * DH), BF16),
+        in_specs=[vmem],
+        out_specs=vmem,
         scratch_shapes=[
-            pltpu.SemaphoreType.DMA,
-            pltpu.SemaphoreType.DMA((pairs,)),
-            pltpu.SemaphoreType.DMA((pairs,)),
+            pltpu.VMEM((rows, 2 * DH), BF16),
+            pltpu.VMEM((rows, DH), F32),
+            pltpu.VMEM((rows, DH), F32),
+            pltpu.VMEM((rows, DH), F32),
+            pltpu.VMEM((pairs, tok, DH), BF16),
+            dma,
+            dma((parts,)),
+            dma((parts,)),
+            dma((pairs,)),
+            dma((pairs,)),
         ],
-        compiler_params=pltpu.CompilerParams(collective_id=1, has_side_effects=True),
-    )(result)
+        compiler_params=pltpu.CompilerParams(
+            collective_id=1, has_side_effects=True, vmem_limit_bytes=32 * 2**20
+        ),
+    )(projected)
 
 
 def local_pairs(features, short_taps, long_filter, skip, norm_gain, w_qkv):
@@ -553,20 +681,18 @@
     taps = short_taps.shape[0]
     tok = features.shape[2]
     width = features.shape[1] // ranks
-    coef = jnp.concatenate([short_taps.reshape(taps * 3, -1), skip[None]], axis=0)
-    coef = lax.dynamic_slice_in_dim(coef, me * width, width, 1).T
-    rows = w_qkv.shape[0]
-    wts = jnp.transpose(w_qkv.reshape(rows, 3, pairs, DH), (2, 0, 1, 3)).reshape(
-        pairs, rows, 3 * DH
-    )
-    gathered, w_all = hyena(
-        features, long_filter.astype(BF16), wts, coef, ranks // 4, taps
-    )
+    taps_here = lax.dynamic_slice_in_dim(short_taps, me * width, width, 2)
+    skip_here = lax.dynamic_slice_in_dim(skip, me * width, width, 0)
+    coef = jnp.concatenate([taps_here.reshape(taps * 3, width), skip_here[None]], axis=0).T
+    coef = jnp.pad(coef, ((0, 0), (0, DH - coef.shape[1])))
+    gathered, w_all = hyena(features, long_filter, w_qkv, coef, ranks // 4, taps)
     channels = norm_gain.shape[0]
     whole = gathered.reshape(channels, pairs * tok)
     half = lax.dynamic_slice(
-        whole, (core * (channels // 2), (me // 2) * tok), (channels // 2, tok)
-    )
+        gathered,
+        (core, 0, 0, 0, (me // 2) * tok),
+        (1, pairs, 2, width, tok),
+    ).reshape(channels // 2, tok)
     whole_f = whole.astype(F32)
     inverse = lax.rsqrt(jnp.mean(whole_f * whole_f, axis=0, keepdims=True) + 1e-06)
     normed = (whole_f * inverse * norm_gain[:, None]).astype(BF16)
@@ -574,18 +700,7 @@
         normed, w_all.reshape(channels, 3 * DH), (((0,), (0,)), ((), ())),
         preferred_element_type=F32,
     ).astype(BF16)
-    mine = projected[:, DH:]
-    other = lax.ppermute(mine, "ctx", [(i, i ^ 1) for i in range(ranks)])
-    mine = mine.reshape(pairs, 1, tok, 2 * DH)
-    other = other.reshape(pairs, 1, tok, 2 * DH)
-    even = jnp.where(x == 0, mine, other)
-    odd = jnp.where(x == 0, other, mine)
-    keyvals = jnp.concatenate([even, odd], axis=1).reshape(ranks * tok, 2 * DH)
-    source = jnp.arange(pairs * tok, dtype=jnp.int32)
-    query_pos = (source // tok * 2 + x) * tok + source % tok
-    result = attend_rows(projected[:, :DH], query_pos, keyvals, 1, ranks * tok)
-    back = give_back(result.astype(BF16).reshape(pairs, tok, DH))
-    attended = jnp.transpose(back, (1, 0, 2)).reshape(tok, pairs * DH)
+    attended = attend(projected, pairs, tok)
     return (half, attended)
 
 

time: 147 us -> 131 us (0.89)
  waiting for transfers between devices: 12.3 us -> 0 us
  Pallas kernels: 106 us -> 114 us
  matrix products: 7.75 us -> 2.4 us
  other arithmetic: 7.12 us -> 2.01 us
    ppermute x1 -> x0, waiting for transfers between devices: 12.3 us -> none  [local_pairs(): other = lax.ppermute(mine, 'ctx', [(i, i ^ 1) for i in range(ranks)])]
    pallas_call x1, Pallas kernels: 26.1 us -> 33.6 us  [attend(): pl.pallas_call(functools.partial(attend_kernel, pairs, tok), out_shape=ja...]
    dot_general x2 -> x0, matrix products: 5.35 us -> none  [the longest x1 3.61 us: step(): jnp.dot(expo.astype(jnp.bfloat16), vals, preferred_element_type=jnp.float32)]
    reduce_sum x1 -> x0, other arithmetic: 3.07 us -> none  [step(): total = total * factor + jnp.sum(expo, axis=1)]
  transfers between devices with their start and end apart: 1 -> 0, of which waited for: 1 -> 0; matrix products, arithmetic and copies ran while one was open for 1% -> 0% of each run, Pallas kernels for 0% -> 0%
where the time goes in v2:
time: 131 us; the launch traced here: 130 us
  Pallas kernels  114 us (87%)
  local copies, waits for them, and re-layouts  10.8 us (8%)
  matrix products  2.4 us (2%)
  other arithmetic  2.01 us (2%)
    pallas_call x1, Pallas kernels, hyena(): pl.pallas_call(functools.partial(hyena_kernel, (ranks, nz, taps)), out_sh...  80 us
    pallas_call x1, Pallas kernels, attend(): pl.pallas_call(functools.partial(attend_kernel, pairs, tok), out_shape=ja...  33.6 us
    unnamed x16, local copies, waits for them, and re-layouts  8.25 us

profile of v2, /device:TPU:0, one launch (start us, length us, event | category | flops | bytes accessed | tf_op | source)
XLA Modules:
  0.0 129.5 jit_solution(3547000622323746021)
XLA Ops:
  0.6 0.0 copy-start
  0.7 0.8 dynamic-slice_bitcast_fusion
  1.5 0.1 copy-done
  1.5 0.1 constant_dynamic-slice_fusion.1
  1.6 0.8 mul.36
  2.4 0.1 copy.20
  2.5 1.8 %copy.21.w_in = bf16[128,3,1024]{2,1,0:T(4,128)(2,1)S(1)} copy(bf16[128,3,1024]{2,0,1:T(8,128)(2,1)} %param.15) | data formatting | bytes 1572864 | tf_op args[5]
  4.3 0.0 copy-start.1
  4.3 1.1 copy-done.1
  5.5 0.0 copy-start.2
  5.5 1.0 copy-done.2
  6.5 0.0 copy-start.3
  6.5 0.9 copy-done.3
  7.4 0.0 copy-start.4
  7.4 0.9 copy-done.4
  8.3 0.8 copy-done.5
  9.2 0.8 copy-done.6
  10.0 80.0 %shard_map.113 = (bf16[2,8,2,64,1024]{4,3,2,1,0:T(8,128)(2,1)S(1)}, bf16[8,2,128,384]{3,2,1,0:T(8,128)(2,1)S(1)}) custom-call(bf16[3,1024,128]{2,1,0:T(8,128)(2,1)S(1)} %copy-done.1, f32[1024,128]{1,0:T(8,128)S(1)} %copy-done.2, bf16[128,3,1024]{2,1,0:T(4,128)(2,1)S(1)} %copy.21.w_in, f32[64,128]{1,0:T(8,128)S(1)} %pad.4.coef_in, ...), custom_call_target="tpu_custom_call" | custom-call | tf_op jit(solution)/shard_map/pallas_call | solution.py:497
  90.0 0.9 fusion
  90.9 0.8 constant_dynamic-slice_fusion
  91.7 1.1 fusion.2
  92.8 2.4 %convolution_convert_fusion.proj = bf16[1024,384]{1,0:T(8,128)(2,1)S(1)} fusion(bf16[2048,1024]{1,0:T(8,128)(2,1)S(1)} %bitcast.9, bf16[2048,384]{1,0:T(8,128)(2,1)S(1)} %bitcast.8), kind=kOutput, calls=%fused_computation.5 | convolution fusion | flops 1611005952 | bytes 6553600 | tf_op jit(solution)/shard_map/dot_general | solution.py:699
  95.2 33.6 %shard_map.114 = bf16[128,1024]{1,0:T(8,128)(2,1)S(1)} custom-call(bf16[1024,384]{1,0:T(8,128)(2,1)S(1)} %convolution_convert_fusion.proj), custom_call_target="tpu_custom_call" | custom-call | tf_op jit(solution)/shard_map/pallas_call | solution.py:652
  128.8 0.7 copy.23
  (7 shorter events, 0.1 us)
Async XLA Ops:
  0.6 0.9 copy-start
  4.3 1.1 copy-start.1
  5.5 1.0 copy-start.2
  6.5 0.9 copy-start.3
  7.4 0.9 copy-start.4
  8.3 0.8 copy-start.5
  9.2 0.8 copy-start.6

commit v3 on v2

--- a/solution.py
+++ b/solution.py
@@ -182,7 +182,7 @@
 def split_table(table):
     high = table.astype(ml_dtypes.bfloat16)
     low = (table - high.astype(np.float64)).astype(ml_dtypes.bfloat16)
-    return jnp.asarray(high), jnp.asarray(low)
+    return [high, low]
 
 
 def packed_tables(tok):
@@ -201,7 +201,7 @@
     imag = -2.0 * np.sin(angle)
     imag[0] = (-1.0) ** np.arange(full)
     backward = np.concatenate([real, imag], axis=0) / full
-    return split_table(forward) + split_table(backward)
+    return np.concatenate(split_table(forward) + split_table(backward), axis=0)
 
 
 def hyena_kernel(
@@ -210,10 +210,7 @@
     filt_in,
     w_in,
     coef_in,
-    fwd_hi_in,
-    fwd_lo_in,
-    inv_hi_in,
-    inv_lo_in,
+    tables_in,
     gathered,
     w_all,
     filt_wide,
@@ -221,10 +218,11 @@
     w_raw,
     wts,
     coef,
-    fwd_hi,
-    fwd_lo,
-    inv_hi,
-    inv_lo,
+    wide_coef,
+    spec_hi,
+    spec_lo,
+    waves,
+    tables,
     feat_all,
     filt_all,
     short0,
@@ -306,10 +304,7 @@
                 (filt_in, filt_wide),
                 (w_in, w_raw),
                 (coef_in, coef),
-                (fwd_hi_in, fwd_hi),
-                (fwd_lo_in, fwd_lo),
-                (inv_hi_in, inv_hi),
-                (inv_lo_in, inv_lo),
+                (tables_in, tables),
             )
         )
     ]
@@ -337,6 +332,8 @@
     own[2].start()
     for load in loads[2:]:
         load.wait()
+    for i in range(3 * taps + 1):
+        wide_coef[i] = jnp.broadcast_to(coef[:, i : i + 1], (width, tok))
     own[0].wait()
     own[1].wait()
     for d in range(1, ranks):
@@ -345,7 +342,6 @@
         w_copy(d).start()
 
     lane = lax.broadcasted_iota(jnp.int32, (width, tok), 1)
-    first = lane == 0
 
     def short_block(b, _):
         before = jnp.maximum(b - 1, 0)
@@ -354,40 +350,53 @@
         for i in range(3):
             now = feat_all[b, i].astype(F32)
             past = feat_all[before, i].astype(F32) * live
-            total = coef[:, i : i + 1] * now
+            total = wide_coef[i] * now
             for lag in range(1, taps):
-                moved = jnp.where(
-                    lane < lag, pltpu.roll(past, lag, 1), pltpu.roll(now, lag, 1)
-                )
-                total = total + coef[:, lag * 3 + i : lag * 3 + i + 1] * moved
+                moved = pltpu.roll(jnp.where(lane < tok - lag, now, past), lag, 1)
+                total = total + wide_coef[lag * 3 + i] * moved
             sums.append(total)
         short0[b] = sums[0]
-        held = (sums[1] * sums[2]).astype(BF16)
-        carried[b] = held
-        spec_x[b] = jnp.dot(held, fwd_hi[...], preferred_element_type=F32) + jnp.dot(
-            held, fwd_lo[...], preferred_element_type=F32
-        )
+        carried[b] = (sums[1] * sums[2]).astype(BF16)
         return 0
 
     lax.fori_loop(0, ranks, short_block, 0)
+
+    group = 4
+    fwd_hi = tables.at[pl.ds(0, tok)]
+    fwd_lo = tables.at[pl.ds(tok, tok)]
+    inv_hi = tables.at[pl.ds(2 * tok, 2 * tok)]
+    inv_lo = tables.at[pl.ds(4 * tok, 2 * tok)]
+
+    def spectra(blocks):
+        rows = blocks.reshape(group * width, tok)
+        spec = jnp.dot(rows, fwd_hi[...], preferred_element_type=F32) + jnp.dot(
+            rows, fwd_lo[...], preferred_element_type=F32
+        )
+        return spec.reshape(group, width, 2 * tok)
+
+    def data_group(g, _):
+        here = pl.ds(g * group, group)
+        spec_x[here] = spectra(carried[here])
+        return 0
+
+    lax.fori_loop(0, ranks // group, data_group, 0)
     for d in range(1, ranks):
         filt_copy(d).wait_recv()
 
-    def filter_block(b, _):
-        lags = filt_all[b]
-        spec = jnp.dot(lags, fwd_hi[...], preferred_element_type=F32) + jnp.dot(
-            lags, fwd_lo[...], preferred_element_type=F32
-        )
-        real = spec[:, :tok]
-        imag = spec[:, tok:]
-        spec_f[b, 0] = real
-        spec_f[b, 1] = jnp.where(first, 0.0, imag)
-        spec_f[b, 2] = jnp.where(first, imag, real)
+    def filter_group(g, _):
+        here = pl.ds(g * group, group)
+        spec = spectra(filt_all[here])
+        real = spec[:, :, :tok]
+        imag = spec[:, :, tok:]
+        zero = lax.broadcasted_iota(jnp.int32, imag.shape, 2) == 0
+        spec_f[here, 0] = real
+        spec_f[here, 1] = jnp.where(zero, 0.0, imag)
+        spec_f[here, 2] = jnp.where(zero, imag, real)
         return 0
 
-    lax.fori_loop(0, ranks, filter_block, 0)
-
-    def block(m, tail):
+    lax.fori_loop(0, ranks // group, filter_group, 0)
+
+    def block(m, _):
         def term(d, acc):
             real, imag = acc
             xr = spec_x[m - d, :, :tok]
@@ -399,21 +408,37 @@
 
         zero = jnp.zeros((width, tok), F32)
         real, imag = lax.fori_loop(0, m + 1, term, (zero, zero))
-        spec = jnp.concatenate([real, imag], axis=1)
-        high = spec.astype(BF16)
-        low = (spec - high.astype(F32)).astype(BF16)
+        rows = pl.ds(pl.multiple_of(m * width, width), width)
+        for at, part in enumerate((real, imag)):
+            high = part.astype(BF16)
+            spec_hi[rows, at * tok : (at + 1) * tok] = high
+            spec_lo[rows, at * tok : (at + 1) * tok] = (part - high.astype(F32)).astype(BF16)
+        return 0
+
+    lax.fori_loop(0, ranks, block, 0)
+
+    def inverse_group(g, _):
+        rows = pl.ds(pl.multiple_of(g * group * width, group * width), group * width)
+        high = spec_hi[rows]
         wave = (
             jnp.dot(high, inv_hi[...], preferred_element_type=F32)
-            + jnp.dot(low, inv_hi[...], preferred_element_type=F32)
+            + jnp.dot(spec_lo[rows], inv_hi[...], preferred_element_type=F32)
             + jnp.dot(high, inv_lo[...], preferred_element_type=F32)
         )
-        long_out = (wave[:, :tok] + tail).astype(BF16).astype(F32)
-        skip = coef[:, 3 * taps : 3 * taps + 1]
-        value = short0[m] * (long_out + skip * carried[m].astype(F32))
+        waves[pl.ds(g * group, group)] = wave.reshape(group, width, 2 * tok)
+        return 0
+
+    lax.fori_loop(0, ranks // group, inverse_group, 0)
+
+    def finish(m, _):
+        live = jnp.where(m > 0, 1.0, 0.0).astype(F32)
+        tail = waves[jnp.maximum(m - 1, 0), :, tok:] * live
+        long_out = (waves[m, :, :tok] + tail).astype(BF16).astype(F32)
+        value = short0[m] * (long_out + wide_coef[3 * taps] * carried[m].astype(F32))
         mixed[m % 2, :, pl.ds(pl.multiple_of((m // 2) * tok, tok), tok)] = value.astype(BF16)
-        return wave[:, tok:]
-
-    lax.fori_loop(0, ranks, block, jnp.zeros((width, tok), F32))
+        return 0
+
+    lax.fori_loop(0, ranks, finish, 0)
 
     keep = pltpu.make_async_copy(mixed.at[x], gathered.at[core, pair, x], local_sem.at[3])
     keep.start()
@@ -428,28 +453,52 @@
     def chunk(p):
         return gathered.at[core, p]
 
-    def z_copy(d):
-        to = (z + d) % nz
+    def up_copy(hop):
+        p = (z - hop) * 2 + y
         return remote(
-            chunk(pair), chunk(pair), z_send.at[d], z_recv.at[d], to * 4 + y * 2 + x, core
-        )
-
-    def y_copy(d):
-        p = ((z - d + nz) % nz) * 2 + y
+            chunk(p), chunk(p), z_send.at[hop], z_recv.at[hop + 1],
+            (z + 1) * 4 + y * 2 + x, core,
+        )
+
+    def down_copy(hop):
+        p = (z + hop) * 2 + y
         return remote(
-            chunk(p), chunk(p), y_send.at[d], y_recv.at[d], z * 4 + (1 - y) * 2 + x, core
-        )
-
-    def s_copy(d, side):
-        p = ((z - d + nz) % nz) * 2 + jnp.where(side == 0, y, 1 - y)
+            chunk(p), chunk(p), z_send.at[nz + hop], z_recv.at[nz + hop + 1],
+            (z - 1) * 4 + y * 2 + x, core,
+        )
+
+    def y_copy(origin):
+        p = origin * 2 + y
         return remote(
-            chunk(p), chunk(p), s_send.at[side * nz + d], s_recv.at[side * nz + d], me, 1 - core
-        )
-
-    y_copy(0).start()
-    for d in range(1, nz):
-        z_copy(d).start()
-    s_copy(0, 0).start()
+            chunk(p), chunk(p), y_send.at[origin], y_recv.at[origin],
+            z * 4 + (1 - y) * 2 + x, core,
+        )
+
+    def s_copy(origin, side):
+        p = origin * 2 + jnp.where(side == 0, y, 1 - y)
+        return remote(
+            chunk(p), chunk(p), s_send.at[side * nz + origin], s_recv.at[side * nz + origin],
+            me, 1 - core,
+        )
+
+    def arrived(hop, up):
+        p = (z - hop if up else z + hop) * 2 + y
+        at = hop if up else nz + hop
+        remote(
+            chunk(p), chunk(p), z_send.at[0], z_recv.at[at],
+            (z - 1 if up else z + 1) * 4 + y * 2 + x, core,
+        ).wait_recv()
+
+    @pl.when(z < nz - 1)
+    def _():
+        up_copy(0).start()
+
+    @pl.when(z > 0)
+    def _():
+        down_copy(0).start()
+
+    y_copy(z).start()
+    s_copy(z, 0).start()
 
     own[2].wait()
     for d in range(1, pairs):
@@ -459,16 +508,47 @@
     )
     w_swap.start()
 
-    for d in range(1, nz):
-        z_copy(d).wait_recv()
-        y_copy(d).start()
-        s_copy(d, 0).start()
-    for d in range(nz):
-        y_copy(d).wait_recv()
-        s_copy(d, 1).start()
-    for d in range(nz):
-        s_copy(d, 0).wait_recv()
-        s_copy(d, 1).wait_recv()
+    for hop in range(1, nz):
+
+        @pl.when(z - hop >= 0)
+        def _():
+            arrived(hop, True)
+
+            @pl.when(z < nz - 1)
+            def _():
+                up_copy(hop).start()
+
+            y_copy(z - hop).start()
+            s_copy(z - hop, 0).start()
+
+        @pl.when(z + hop < nz)
+        def _():
+            arrived(hop, False)
+
+            @pl.when(z > 0)
+            def _():
+                down_copy(hop).start()
+
+            y_copy(z + hop).start()
+            s_copy(z + hop, 0).start()
+
+    for hop in range(nz):
+
+        @pl.when(z - hop >= 0)
+        def _():
+            y_copy(z - hop).wait_recv()
+            s_copy(z - hop, 1).start()
+
+        if hop > 0:
+
+            @pl.when(z + hop < nz)
+            def _():
+                y_copy(z + hop).wait_recv()
+                s_copy(z + hop, 1).start()
+
+    for origin in range(nz):
+        s_copy(origin, 0).wait_recv()
+        s_copy(origin, 1).wait_recv()
     w_swap.wait()
     for d in range(1, ranks):
         feat_copy(d).wait_send()
@@ -476,12 +556,20 @@
     for d in range(1, pairs):
         w_copy(d).wait_send()
     swap.wait_send()
-    for d in range(1, nz):
-        z_copy(d).wait_send()
-    for d in range(nz):
-        y_copy(d).wait_send()
-        s_copy(d, 0).wait_send()
-        s_copy(d, 1).wait_send()
+    for hop in range(nz):
+
+        @pl.when((z < nz - 1) & (z - hop >= 0))
+        def _():
+            up_copy(hop).wait_send()
+
+        @pl.when((z > 0) & (z + hop < nz))
+        def _():
+            down_copy(hop).wait_send()
+
+    for origin in range(nz):
+        y_copy(origin).wait_send()
+        s_copy(origin, 0).wait_send()
+        s_copy(origin, 1).wait_send()
 
 
 def hyena(features, filt, w_qkv, coef, nz, taps):
@@ -491,7 +579,7 @@
     pairs = ranks // 2
     rows = w_qkv.shape[0]
     columns = 3 * DH
-    tables = packed_tables(tok)
+    tables = jnp.asarray(packed_tables(tok))
     hbm = pl.BlockSpec(memory_space=pl.ANY)
     dma = pltpu.SemaphoreType.DMA
     return pl.pallas_call(
@@ -500,7 +588,7 @@
             jax.ShapeDtypeStruct((2, pairs, 2, width, pairs * tok), BF16),
             jax.ShapeDtypeStruct((pairs, 2, rows, columns), BF16),
         ),
-        in_specs=[hbm] * 8,
+        in_specs=[hbm] * 5,
         out_specs=(hbm, hbm),
         scratch_shapes=[
             pltpu.VMEM(filt.shape, F32),
@@ -508,8 +596,12 @@
             pltpu.VMEM(w_qkv.shape, BF16),
             pltpu.VMEM((pairs, rows, columns), BF16),
             pltpu.VMEM(coef.shape, F32),
+            pltpu.VMEM((3 * taps + 1, width, tok), F32),
+            pltpu.VMEM((ranks * width, 2 * tok), BF16),
+            pltpu.VMEM((ranks * width, 2 * tok), BF16),
+            pltpu.VMEM((ranks, width, 2 * tok), F32),
         ]
-        + [pltpu.VMEM(table.shape, BF16) for table in tables]
+        + [pltpu.VMEM(tables.shape, BF16)]
         + [
             pltpu.VMEM((ranks, 3, width, tok), BF16),
             pltpu.VMEM((ranks, width, tok), BF16),
@@ -518,7 +610,7 @@
             pltpu.VMEM((ranks, width, 2 * tok), F32),
             pltpu.VMEM((ranks, 3, width, tok), F32),
             pltpu.VMEM((2, width, pairs * tok), BF16),
-            dma((11,)),
+            dma((8,)),
             dma((ranks,)),
             dma((ranks,)),
             dma((ranks,)),
@@ -529,17 +621,17 @@
             dma((1,)),
             dma((1,)),
             dma((1,)),
-            dma((nz,)),
-            dma((nz,)),
+            dma((2 * nz,)),
+            dma((2 * nz,)),
             dma((nz,)),
             dma((nz,)),
             dma((2 * nz,)),
             dma((2 * nz,)),
         ],
         compiler_params=pltpu.CompilerParams(
-            collective_id=0, has_side_effects=True, vmem_limit_bytes=32 * 2**20
+            collective_id=0, has_side_effects=True, vmem_limit_bytes=60 * 2**20
         ),
-    )(features, filt, w_qkv, coef, *tables)
+    )(features, filt, w_qkv, coef, tables)
 
 
 def attend_kernel(

time: 131 us -> 114 us (0.87)
  Pallas kernels: 114 us -> 96.7 us
  local copies, waits for them, and re-layouts: 10.8 us -> 7.22 us
  other arithmetic: 2.01 us -> 4.37 us
    pallas_call x1, Pallas kernels: 33.6 us -> 17.4 us  [attend(): pl.pallas_call(functools.partial(attend_kernel, pairs, tok), out_shape=ja...]
    unnamed x16 -> x8, local copies, waits for them, and re-layouts: 8.25 us -> 4.07 us
    reduce_sum x1, other arithmetic: 0.92 us -> 3.27 us  [local_pairs(): jnp.mean(whole_f * whole_f, axis=0, keepdims=True) + 1e-06]
where the time goes in v3:
time: 114 us; the launch traced here: 111 us
  Pallas kernels  96.7 us (85%)
  local copies, waits for them, and re-layouts  7.22 us (6%)
  other arithmetic  4.37 us (4%)
  matrix products  2.36 us (2%)
    pallas_call x1, Pallas kernels, hyena(): pl.pallas_call(functools.partial(hyena_kernel, (ranks, nz, taps)), out_sh...  79.3 us
    pallas_call x1, Pallas kernels, attend(): pl.pallas_call(functools.partial(attend_kernel, pairs, tok), out_shape=ja...  17.4 us
    unnamed x8, local copies, waits for them, and re-layouts  4.07 us
    reduce_sum x1, other arithmetic, local_pairs(): jnp.mean(whole_f * whole_f, axis=0, keepdims=True) + 1e-06  3.27 us
    dot_general x1, matrix products, local_pairs(): lax.dot_general(normed, w_all.reshape(channels, 3 * DH), (((0,), (0,)), (...  2.36 us

profile of v3, /device:TPU:0, one launch (start us, length us, event | category | flops | bytes accessed | tf_op | source)
XLA Modules:
  0.0 111.4 jit_solution(4219553209832508350)
XLA Ops:
  0.6 0.0 copy-start
  0.7 0.8 dynamic-slice_bitcast_fusion
  1.5 0.1 copy-done
  1.5 0.1 constant_dynamic-slice_fusion.1
  1.6 0.8 mul.36
  2.4 0.1 copy.17
  2.5 0.6 pad.4.coef_in
  3.1 2.8 %copy.18.w_in = bf16[128,3,1024]{2,1,0:T(4,128)(2,1)} copy(bf16[128,3,1024]{2,0,1:T(8,128)(2,1)} %param.12) | data formatting | bytes 1572864 | tf_op args[5]
  5.9 79.3 %shard_map.86 = (bf16[2,8,2,64,1024]{4,3,2,1,0:T(8,128)(2,1)}, bf16[8,2,128,384]{3,2,1,0:T(8,128)(2,1)}) custom-call(bf16[3,1024,128]{2,1,0:T(8,128)(2,1)} %feats.1, f32[1024,128]{1,0:T(8,128)} %filt_in.1, bf16[128,3,1024]{2,1,0:T(4,128)(2,1)} %copy.18.w_in, f32[64,128]{1,0:T(8,128)} %pad.4.coef_in, bf16[768,256]{1,0:T(8,128)(2,1)} %constant.40.clone.tables_in), custom_call_target="tpu_custom_call" | custom-call | tf_op jit(solution)/shard_map/pallas_call | solution.py:585
  85.3 0.0 copy-start.1
  85.3 3.3 %fusion = f32[1024]{0:T(1024)S(1)} fusion(bf16[2,8,2,64,1024]{4,3,2,1,0:T(8,128)(2,1)} %get-tuple-element.4), kind=kLoop, calls=%fused_computation.2 | loop fusion | flops 6290432 | bytes 4198400 | tf_op jit(solution)/shard_map/reduce_sum | solution.py:789
  88.6 0.2 copy-done.1
  88.7 0.8 constant_dynamic-slice_fusion
  89.5 0.0 copy-start.2
  89.5 1.1 fusion.2
  90.6 0.3 copy-done.2
  90.9 2.4 %convolution_convert_fusion.proj = bf16[1024,384]{1,0:T(8,128)(2,1)S(1)} fusion(bf16[2048,1024]{1,0:T(8,128)(2,1)S(1)} %bitcast.8, bf16[2048,384]{1,0:T(8,128)(2,1)S(1)} %bitcast.11), kind=kOutput, calls=%fused_computation.5 | convolution fusion | flops 1611005952 | bytes 6553600 | tf_op jit(solution)/shard_map/dot_general | solution.py:791
  93.3 17.4 %shard_map.87 = bf16[128,1024]{1,0:T(8,128)(2,1)S(1)} custom-call(bf16[1024,384]{1,0:T(8,128)(2,1)S(1)} %convolution_convert_fusion.proj), custom_call_target="tpu_custom_call" | custom-call | tf_op jit(solution)/shard_map/pallas_call | solution.py:744
  110.7 0.7 copy.20
  (4 shorter events, 0.0 us)
Async XLA Ops:
  0.6 0.9 copy-start
  85.3 3.5 %copy-start.1 = (bf16[2,8,2,64,1024]{4,3,2,1,0:T(8,128)(2,1)S(1)}, bf16[2,8,2,64,1024]{4,3,2,1,0:T(8,128)(2,1)}, u32[]{:S(2)}) copy-start(bf16[2,8,2,64,1024]{4,3,2,1,0:T(8,128)(2,1)} %get-tuple-element.4) | copy-start | bytes 12582916
  89.5 1.4 %copy-start.2 = (bf16[8,2,128,384]{3,2,1,0:T(8,128)(2,1)S(1)}, bf16[8,2,128,384]{3,2,1,0:T(8,128)(2,1)}, u32[]{:S(2)}) copy-start(bf16[8,2,128,384]{3,2,1,0:T(8,128)(2,1)} %get-tuple-element.5) | copy-start | bytes 4718596

commit v4 on v3

--- a/solution.py
+++ b/solution.py
@@ -328,7 +328,7 @@
     loads[1].wait()
     for i in range(3):
         for h in range(pairs):
-            wts[h, :, i * DH : (i + 1) * DH] = w_raw[:, i, h * DH : (h + 1) * DH]
+            wts[h, :, i * DH : (i + 1) * DH] = w_raw[i, :, h * DH : (h + 1) * DH]
     own[2].start()
     for load in loads[2:]:
         load.wait()
@@ -577,7 +577,7 @@
     width = coef.shape[0]
     tok = features.shape[2]
     pairs = ranks // 2
-    rows = w_qkv.shape[0]
+    rows = w_qkv.shape[1]
     columns = 3 * DH
     tables = jnp.asarray(packed_tables(tok))
     hbm = pl.BlockSpec(memory_space=pl.ANY)
@@ -777,7 +777,8 @@
     skip_here = lax.dynamic_slice_in_dim(skip, me * width, width, 0)
     coef = jnp.concatenate([taps_here.reshape(taps * 3, width), skip_here[None]], axis=0).T
     coef = jnp.pad(coef, ((0, 0), (0, DH - coef.shape[1])))
-    gathered, w_all = hyena(features, long_filter, w_qkv, coef, ranks // 4, taps)
+    stacked = jnp.transpose(w_qkv, (1, 0, 2))
+    gathered, w_all = hyena(features, long_filter, stacked, coef, ranks // 4, taps)
     channels = norm_gain.shape[0]
     whole = gathered.reshape(channels, pairs * tok)
     half = lax.dynamic_slice(

time: 114 us -> 111 us (0.974)
  local copies, waits for them, and re-layouts: 7.22 us -> 4.42 us
    unnamed x8 -> x7, local copies, waits for them, and re-layouts: 4.07 us -> 1.27 us
where the time goes in v4:
time: 111 us; the launch traced here: 109 us
  Pallas kernels  96.7 us (87%)
  local copies, waits for them, and re-layouts  4.42 us (4%)
  other arithmetic  4.37 us (4%)
  matrix products  2.36 us (2%)
    pallas_call x1, Pallas kernels, hyena(): pl.pallas_call(functools.partial(hyena_kernel, (ranks, nz, taps)), out_sh...  79.3 us
    pallas_call x1, Pallas kernels, attend(): pl.pallas_call(functools.partial(attend_kernel, pairs, tok), out_shape=ja...  17.4 us
    reduce_sum x1, other arithmetic, local_pairs(): jnp.mean(whole_f * whole_f, axis=0, keepdims=True) + 1e-06  3.27 us
    dot_general x1, matrix products, local_pairs(): lax.dot_general(normed, w_all.reshape(channels, 3 * DH), (((0,), (0,)), (...  2.36 us

profile of v4, /device:TPU:0, one launch (start us, length us, event | category | flops | bytes accessed | tf_op | source)
XLA Modules:
  0.0 108.6 jit_solution(7202163104367751613)
XLA Ops:
  0.6 0.0 copy-start
  0.7 0.8 dynamic-slice_bitcast_fusion
  1.5 0.1 copy-done
  1.5 0.1 constant_dynamic-slice_fusion.1
  1.6 0.8 mul.36
  2.4 0.1 copy.15
  2.5 0.6 pad.4.coef_in
  3.1 79.3 %shard_map.86 = (bf16[2,8,2,64,1024]{4,3,2,1,0:T(8,128)(2,1)}, bf16[8,2,128,384]{3,2,1,0:T(8,128)(2,1)}) custom-call(bf16[3,1024,128]{2,1,0:T(8,128)(2,1)} %feats.1, f32[1024,128]{1,0:T(8,128)} %filt_in.1, bf16[3,128,1024]{2,1,0:T(8,128)(2,1)} %bitcast.10, f32[64,128]{1,0:T(8,128)} %pad.4.coef_in, bf16[768,256]{1,0:T(8,128)(2,1)} %constant.40.clone.tables_in), custom_call_target="tpu_custom_call" | custom-call | tf_op jit(solution)/shard_map/pallas_call | solution.py:585
  82.5 0.0 copy-start.1
  82.5 3.3 %fusion = f32[1024]{0:T(1024)S(1)} fusion(bf16[2,8,2,64,1024]{4,3,2,1,0:T(8,128)(2,1)} %get-tuple-element.4), kind=kLoop, calls=%fused_computation.2 | loop fusion | flops 6290432 | bytes 4198400 | tf_op jit(solution)/shard_map/reduce_sum | solution.py:790
  85.8 0.2 copy-done.1
  85.9 0.8 constant_dynamic-slice_fusion
  86.7 0.0 copy-start.2
  86.7 1.1 fusion.2
  87.8 0.3 copy-done.2
  88.1 2.4 %convolution_convert_fusion.proj = bf16[1024,384]{1,0:T(8,128)(2,1)S(1)} fusion(bf16[2048,1024]{1,0:T(8,128)(2,1)S(1)} %bitcast.9, bf16[2048,384]{1,0:T(8,128)(2,1)S(1)} %bitcast.13), kind=kOutput, calls=%fused_computation.5 | convolution fusion | flops 1611005952 | bytes 6553600 | tf_op jit(solution)/shard_map/dot_general | solution.py:792
  90.5 17.4 %shard_map.87 = bf16[128,1024]{1,0:T(8,128)(2,1)S(1)} custom-call(bf16[1024,384]{1,0:T(8,128)(2,1)S(1)} %convolution_convert_fusion.proj), custom_call_target="tpu_custom_call" | custom-call | tf_op jit(solution)/shard_map/pallas_call | solution.py:744
  107.9 0.7 copy.17
  (4 shorter events, 0.0 us)
Async XLA Ops:
  0.6 0.9 copy-start
  82.5 3.5 %copy-start.1 = (bf16[2,8,2,64,1024]{4,3,2,1,0:T(8,128)(2,1)S(1)}, bf16[2,8,2,64,1024]{4,3,2,1,0:T(8,128)(2,1)}, u32[]{:S(2)}) copy-start(bf16[2,8,2,64,1024]{4,3,2,1,0:T(8,128)(2,1)} %get-tuple-element.4) | copy-start | bytes 12582916
  86.7 1.4 %copy-start.2 = (bf16[8,2,128,384]{3,2,1,0:T(8,128)(2,1)S(1)}, bf16[8,2,128,384]{3,2,1,0:T(8,128)(2,1)}, u32[]{:S(2)}) copy-start(bf16[8,2,128,384]{3,2,1,0:T(8,128)(2,1)} %get-tuple-element.5) | copy-start | bytes 4718596

commit v5 on v4

--- a/solution.py
+++ b/solution.py
@@ -500,15 +500,15 @@
     y_copy(z).start()
     s_copy(z, 0).start()
 
-    own[2].wait()
-    for d in range(1, pairs):
-        w_copy(d).wait_recv()
-    w_swap = remote(
-        w_all.at[:, x], w_all.at[:, x], wx_send.at[0], wx_recv.at[0], pair * 2 + 1 - x, core
-    )
-    w_swap.start()
-
     for hop in range(1, nz):
+        if hop == 2:
+            own[2].wait()
+            for d in range(1, pairs):
+                w_copy(d).wait_recv()
+            w_swap = remote(
+                w_all.at[:, x], w_all.at[:, x], wx_send.at[0], wx_recv.at[0], pair * 2 + 1 - x, core
+            )
+            w_swap.start()
 
         @pl.when(z - hop >= 0)
         def _():

time: 111 us -> 110 us (level)
  no operation moved by 1% of the time
where the time goes in v5:
time: 110 us; the launch traced here: 108 us
  Pallas kernels  96.5 us (88%)
  local copies, waits for them, and re-layouts  4.42 us (4%)
  other arithmetic  4.37 us (4%)
  matrix products  2.36 us (2%)
    pallas_call x1, Pallas kernels, hyena(): pl.pallas_call(functools.partial(hyena_kernel, (ranks, nz, taps)), out_sh...  79.1 us
    pallas_call x1, Pallas kernels, attend(): pl.pallas_call(functools.partial(attend_kernel, pairs, tok), out_shape=ja...  17.4 us
    reduce_sum x1, other arithmetic, local_pairs(): jnp.mean(whole_f * whole_f, axis=0, keepdims=True) + 1e-06  3.27 us
    dot_general x1, matrix products, local_pairs(): lax.dot_general(normed, w_all.reshape(channels, 3 * DH), (((0,), (0,)), (...  2.36 us

profile of v5, /device:TPU:0, one launch (start us, length us, event | category | flops | bytes accessed | tf_op | source)
XLA Modules:
  0.0 108.4 jit_solution(6155998260060955201)
XLA Ops:
  0.6 0.0 copy-start
  0.7 0.8 dynamic-slice_bitcast_fusion
  1.5 0.1 copy-done
  1.5 0.1 constant_dynamic-slice_fusion.1
  1.6 0.8 mul.36
  2.4 0.1 copy.15
  2.5 0.6 pad.4.coef_in
  3.1 79.1 %shard_map.86 = (bf16[2,8,2,64,1024]{4,3,2,1,0:T(8,128)(2,1)}, bf16[8,2,128,384]{3,2,1,0:T(8,128)(2,1)}) custom-call(bf16[3,1024,128]{2,1,0:T(8,128)(2,1)} %feats.1, f32[1024,128]{1,0:T(8,128)} %filt_in.1, bf16[3,128,1024]{2,1,0:T(8,128)(2,1)} %bitcast.10, f32[64,128]{1,0:T(8,128)} %pad.4.coef_in, bf16[768,256]{1,0:T(8,128)(2,1)} %constant.40.clone.tables_in), custom_call_target="tpu_custom_call" | custom-call | tf_op jit(solution)/shard_map/pallas_call | solution.py:585
  82.3 0.0 copy-start.1
  82.3 3.3 %fusion = f32[1024]{0:T(1024)S(1)} fusion(bf16[2,8,2,64,1024]{4,3,2,1,0:T(8,128)(2,1)} %get-tuple-element.4), kind=kLoop, calls=%fused_computation.2 | loop fusion | flops 6290432 | bytes 4198400 | tf_op jit(solution)/shard_map/reduce_sum | solution.py:790
  85.6 0.2 copy-done.1
  85.7 0.8 constant_dynamic-slice_fusion
  86.5 0.0 copy-start.2
  86.5 1.1 fusion.2
  87.6 0.3 copy-done.2
  87.9 2.4 %convolution_convert_fusion.proj = bf16[1024,384]{1,0:T(8,128)(2,1)S(1)} fusion(bf16[2048,1024]{1,0:T(8,128)(2,1)S(1)} %bitcast.9, bf16[2048,384]{1,0:T(8,128)(2,1)S(1)} %bitcast.13), kind=kOutput, calls=%fused_computation.5 | convolution fusion | flops 1611005952 | bytes 6553600 | tf_op jit(solution)/shard_map/dot_general | solution.py:792
  90.3 17.4 %shard_map.87 = bf16[128,1024]{1,0:T(8,128)(2,1)S(1)} custom-call(bf16[1024,384]{1,0:T(8,128)(2,1)S(1)} %convolution_convert_fusion.proj), custom_call_target="tpu_custom_call" | custom-call | tf_op jit(solution)/shard_map/pallas_call | solution.py:744
  107.7 0.7 copy.17
  (4 shorter events, 0.0 us)
Async XLA Ops:
  0.6 0.9 copy-start
  82.3 3.5 %copy-start.1 = (bf16[2,8,2,64,1024]{4,3,2,1,0:T(8,128)(2,1)S(1)}, bf16[2,8,2,64,1024]{4,3,2,1,0:T(8,128)(2,1)}, u32[]{:S(2)}) copy-start(bf16[2,8,2,64,1024]{4,3,2,1,0:T(8,128)(2,1)} %get-tuple-element.4) | copy-start | bytes 12582916
  86.5 1.4 %copy-start.2 = (bf16[8,2,128,384]{3,2,1,0:T(8,128)(2,1)S(1)}, bf16[8,2,128,384]{3,2,1,0:T(8,128)(2,1)}, u32[]{:S(2)}) copy-start(bf16[8,2,128,384]{3,2,1,0:T(8,128)(2,1)} %get-tuple-element.5) | copy-start | bytes 4718596
